TPU v7x, 32 devices: a whole 2x2x4 slice. The times are simulated.
32 devices in a mesh: section: 2 (over core), dp: 16 (over z, y, x).
Axes of the slice: x: 2, y: 2, z: 4, core: 2. Of those that a mesh axis runs over, the one named last changes fastest.
Arguments:
- entering: bfloat16 [2, 2, 64, 4096], P(None, None, None, 'dp'), may hold values from -6 to 6
- cotangent: bfloat16 [2, 2, 64, 4096], P(None, None, None, 'dp'), may hold values from -6 to 6
- weights: bfloat16 [2, 4096, 4096], P('section', 'dp'), may hold values from -0.09375 to 0.09375
Outputs:
- acts_down: bfloat16 [2, 2, 64, 4096], P('section', None, None, 'dp')
- acts_up: bfloat16 [2, 2, 64, 4096], P('section', None, None, 'dp')
- grads_down: bfloat16 [2, 2, 64, 4096], P('section', None, None, 'dp')
- grads_up: bfloat16 [2, 2, 64, 4096], P('section', None, None, 'dp')
- weight_grad: float32 [2, 4096, 4096], P('section', 'dp')
All inputs are finite; a program needn't handle non-finite values.
Results may differ from a plain program's by a relative error of at most 0.0052.
Values may be sent and summed in bfloat16 or wider, within the bound.
A program may use at most 64 MiB of HBM per device.

v0:
```python
import jax
import jax.numpy as jnp
from jax import lax
from jax.sharding import PartitionSpec as P

NORM_EPS = 1e-05


def for_sending(value):

    def short(part):
        return part.astype(jnp.bfloat16) if part.dtype == jnp.float32 else part

    return jax.tree.map(short, value)


def from_behind(value, axis, steps):
    count = lax.axis_size(axis)
    first, last = (max(0, -steps), min(count, count - steps))
    return lax.ppermute(value, axis, [(source, source + steps) for source in range(first, last)])


def swapped_2(block, axis, apart):
    count = lax.axis_size(axis)
    route = []
    for low in range(count):
        high = low | 1 << apart
        if high != low and high < count:
            route += [(low, high), (high, low)]
    return lax.ppermute(block, axis, route)


def pass_along(payload, ahead):
    if ahead:
        return jax.tree.map(
            lambda part, own: part.astype(own.dtype),
            from_behind(for_sending(payload), "section", 1),
            payload,
        )
    return jax.tree.map(
        lambda part, own: part.astype(own.dtype),
        from_behind(for_sending(payload), "section", -1),
        payload,
    )


def send_pair(down_part, up_part, down_ahead):
    return jnp.stack([pass_along(down_part, down_ahead), pass_along(up_part, not down_ahead)])


def section_bits():
    return lax.axis_size("section").bit_length() - 1


def mirror_weights(payload):
    for bit_idx in range(section_bits()):
        payload = swapped_2(payload, "section", bit_idx)
    return payload


def mirror_grads(payload):
    for bit_idx in range(section_bits()):
        payload = swapped_2(payload.astype(jnp.bfloat16), "section", bit_idx).astype(payload.dtype)
    return payload


def row_totals(first_part, second_part):
    return lax.psum((first_part, second_part), "dp")


def place_slot(store, stream, slot_idx, payload, is_live):
    previous = lax.dynamic_index_in_dim(store[stream], slot_idx, 0, keepdims=False)
    kept = jnp.where(is_live, payload.astype(store.dtype), previous)
    zero_idx = jnp.zeros((), jnp.int32)
    starts = (jnp.int32(stream), slot_idx) + (zero_idx,) * (store.ndim - 2)
    return lax.dynamic_update_slice(store, kept[None, None], starts)


def forward_cols(full_rows, input_cols, weight_cols):
    values = full_rows.astype(jnp.float32)
    row_scale = lax.rsqrt(jnp.mean(values * values, axis=1, keepdims=True) + NORM_EPS)
    normed = (values * row_scale).astype(jnp.bfloat16)
    mixed_cols = jnp.dot(normed, weight_cols, preferred_element_type=jnp.float32)
    output_cols = (input_cols.astype(jnp.float32) + mixed_cols).astype(jnp.bfloat16)
    return (output_cols, normed, mixed_cols, row_scale[:, 0])


def body(entering, cotangent, weights):
    section_count = lax.axis_size("section")
    last_section = section_count - 1
    section_idx = lax.axis_index("section")
    group_count = lax.axis_size("dp")
    local_cols = weights.shape[1]
    model_width = weights.shape[2]
    col_start = lax.axis_index("dp") * local_cols
    micro_count = entering.shape[1]
    tok_rows = entering.shape[2]
    tick_count = micro_count + section_count - 1
    own_rows = weights[0]
    held_rows = jnp.stack([own_rows, mirror_weights(own_rows)])
    up_delay = last_section - section_idx
    held_count = held_rows.shape[0]
    split_rows = held_rows.reshape(held_count, local_cols, group_count, local_cols)
    swapped = lax.all_to_all(split_rows, "dp", split_axis=2, concat_axis=1, tiled=True)
    held_cols = swapped.reshape(held_count, model_width, local_cols)
    held_last = held_count - 1
    fwd_delays = (section_idx, up_delay)
    back_delays = (last_section - section_idx, last_section - up_delay)

    def slot_of(tick_idx, delay_now):
        micro_idx = tick_idx - delay_now
        slot_idx = jnp.clip(micro_idx, 0, micro_count - 1)
        is_live = (micro_idx >= 0) & (micro_idx < micro_count)
        return (slot_idx, is_live)

    def forward_tick(tick_idx, state_now):
        inbox, normed_store, mixed_store, scale_store, act_store = state_now
        inputs_now = []
        slots_now = []
        for stream in range(2):
            slot_idx, is_live = slot_of(tick_idx, fwd_delays[stream])
            fresh = lax.dynamic_index_in_dim(entering[stream], slot_idx, 0, keepdims=False)
            inputs_now.append(jnp.where(fwd_delays[stream] == 0, fresh, inbox[stream]))
            slots_now.append((slot_idx, is_live))
        full_down, full_up = (
            lax.all_gather(for_sending(inputs_now[0]), "dp", axis=1, tiled=True),
            lax.all_gather(for_sending(inputs_now[1]), "dp", axis=1, tiled=True),
        )
        outputs_now = []
        for stream, full_rows in enumerate((full_down, full_up)):
            output_cols, normed, mixed_cols, row_scale = forward_cols(
                full_rows, inputs_now[stream], held_cols[stream * held_last]
            )
            slot_idx, is_live = slots_now[stream]
            normed_store = place_slot(normed_store, stream, slot_idx, normed, is_live)
            mixed_store = place_slot(mixed_store, stream, slot_idx, mixed_cols, is_live)
            scale_store = place_slot(scale_store, stream, slot_idx, row_scale, is_live)
            act_store = place_slot(act_store, stream, slot_idx, output_cols, is_live)
            outputs_now.append(output_cols)
        inbox = send_pair(outputs_now[0], outputs_now[1], True)
        return (inbox, normed_store, mixed_store, scale_store, act_store)

    start_fwd = (
        jnp.zeros((2, tok_rows, local_cols), jnp.bfloat16),
        jnp.zeros((2, micro_count, tok_rows, model_width), jnp.bfloat16),
        jnp.zeros((2, micro_count, tok_rows, local_cols), jnp.float32),
        jnp.zeros((2, micro_count, tok_rows), jnp.float32),
        jnp.zeros((2, micro_count, tok_rows, local_cols), jnp.bfloat16),
    )
    ended_fwd = lax.fori_loop(0, tick_count, forward_tick, start_fwd)
    normed_store, mixed_store, scale_store, act_store = (
        ended_fwd[1],
        ended_fwd[2],
        ended_fwd[3],
        ended_fwd[4],
    )

    def backward_tick(tick_idx, state_now):
        inbox, grad_store, weight_acc = state_now
        slopes_now = []
        picks = []
        for stream in range(2):
            slot_idx, is_live = slot_of(tick_idx, back_delays[stream])
            fresh = lax.dynamic_index_in_dim(cotangent[stream], slot_idx, 0, keepdims=False)
            slopes_now.append(jnp.where(back_delays[stream] == 0, fresh, inbox[stream]))
            normed = lax.dynamic_index_in_dim(normed_store[stream], slot_idx, 0, keepdims=False)
            mixed_cols = lax.dynamic_index_in_dim(mixed_store[stream], slot_idx, 0, keepdims=False)
            row_scale = lax.dynamic_index_in_dim(scale_store[stream], slot_idx, 0, keepdims=False)
            picks.append((slot_idx, is_live, normed, mixed_cols, row_scale))
        slope_down, slope_up = (
            lax.all_gather(for_sending(slopes_now[0]), "dp", axis=1, tiled=True),
            lax.all_gather(for_sending(slopes_now[1]), "dp", axis=1, tiled=True),
        )
        slope_fulls = (slope_down, slope_up)
        back_sums = []
        normed_locals = []
        for stream in range(2):
            back_sums.append(
                lax.dot_general(
                    slope_fulls[stream],
                    held_rows[stream * held_last],
                    (((1,), (1,)), ((), ())),
                    preferred_element_type=jnp.float32,
                )
            )
            normed_locals.append(
                lax.dynamic_slice_in_dim(picks[stream][2], col_start, local_cols, 1)
            )
        row_sums = row_totals(
            jnp.sum(back_sums[0] * normed_locals[0].astype(jnp.float32), axis=1),
            jnp.sum(back_sums[1] * normed_locals[1].astype(jnp.float32), axis=1),
        )
        grads_now = []
        for stream in range(2):
            slot_idx, is_live, normed, mixed_cols, row_scale = picks[stream]
            row_dot = row_sums[stream][:, None]
            normed_part = normed_locals[stream].astype(jnp.float32)
            grad_cols = (
                slopes_now[stream].astype(jnp.float32)
                + row_scale[:, None] * (back_sums[stream] - normed_part * row_dot / model_width)
            ).astype(jnp.bfloat16)
            weight_step = lax.dot_general(
                normed_locals[stream],
                slope_fulls[stream],
                (((0,), (0,)), ((), ())),
                preferred_element_type=jnp.float32,
            )
            weight_acc = weight_acc.at[stream].add(weight_step * is_live.astype(jnp.float32))
            grad_store = place_slot(grad_store, stream, slot_idx, grad_cols, is_live)
            grads_now.append(grad_cols)
        inbox = send_pair(grads_now[0], grads_now[1], False)
        return (inbox, grad_store, weight_acc)

    start_back = (
        jnp.zeros((2, tok_rows, local_cols), jnp.bfloat16),
        jnp.zeros((2, micro_count, tok_rows, local_cols), jnp.bfloat16),
        jnp.zeros((2, local_cols, model_width), jnp.float32),
    )
    ended_back = lax.fori_loop(0, tick_count, backward_tick, start_back)
    grad_store, weight_acc = (ended_back[1], ended_back[2])
    total_grad = weight_acc[0] + mirror_grads(weight_acc[1])
    acts_up = act_store[1]
    grads_up = grad_store[1]
    return (
        act_store[0][None],
        acts_up[None],
        grad_store[0][None],
        grads_up[None],
        total_grad[None],
    )


def solution(mesh):
    placed = (P(None, None, None, "dp"), P(None, None, None, "dp"), P("section", "dp", None))
    return jax.shard_map(
        body,
        mesh=mesh,
        in_specs=placed,
        out_specs=(
            P("section", None, None, "dp"),
            P("section", None, None, "dp"),
            P("section", None, None, "dp"),
            P("section", None, None, "dp"),
            P("section", "dp", None),
        ),
        check_vma=False,
    )
```

profile of v0, /device:TPU:0, one launch (start us, length us, event | category | flops | bytes accessed | tf_op | source)
XLA Modules:
  0.0 849.8 jit_solution(6026896950334336985)
XLA Ops:
  13.2 6.4 copy.11
  19.6 8.3 all-to-all-start
  30.8 77.4 %all-to-all-done = bf16[2,256,16,256]{3,1,0,2:T(8,128)(2,1)} async-done(((bf16[2,256,16,256]{3,1,0,2:T(8,128)(2,1)}), bf16[2,256,16,256]{3,1,0,2:T(8,128)(2,1)}, u32[]{:S(2)}, u32[]{:S(2)}) %all-to-all-start) | async-done | bytes 4194336 | tf_op jit(solution)/shard_map/all_to_all | solution.py:104
  113.2 286.4 %while.42 = (s32[]{:T(128)}, bf16[2,64,256]{2,1,0:T(8,128)(2,1)S(1)}, bf16[2,2,64,4096]{3,2,1,0:T(8,128)(2,1)S(1)}, f32[2,2,64]{2,1,0:T(2,128)S(1)}, bf16[2,2,64...) while((s32[]{:T(128)}, ...), condition=%wide.region_3.4_spmd, body=%wide.region_0.3_spmd.sunk | while | flops 273875456 | bytes 16131475 | solution.py:150
  113.2 55.8 %all_gather.42 = bf16[64,4096]{1,0:T(8,128)(2,1)S(1)} all-gather(bf16[64,256]{1,0:T(8,128)(2,1)S(1)} %get-tuple-element.883), channel_id=1, replica_groups=mesh['section'=2,'dp'=16] {'dp'}, dimensions={1}, use_global_device_ids=true | all-gather | bytes 557056 | tf_op jit(solution)/shard_map/while/body/eval_jaxpr/all_gather | solution.py:126
  173.3 38.5 %all_gather.43 = bf16[64,4096]{1,0:T(8,128)(2,1)S(1)} all-gather(bf16[64,256]{1,0:T(8,128)(2,1)S(1)} %get-tuple-element.885), channel_id=1, replica_groups=mesh['section'=2,'dp'=16] {'dp'}, dimensions={1}, use_global_device_ids=true | all-gather | bytes 557056 | tf_op jit(solution)/shard_map/while/body/eval_jaxpr/all_gather | solution.py:127
  218.9 40.5 %all_gather.42 = bf16[64,4096]{1,0:T(8,128)(2,1)S(1)} all-gather(bf16[64,256]{1,0:T(8,128)(2,1)S(1)} %get-tuple-element.883), channel_id=1, replica_groups=mesh['section'=2,'dp'=16] {'dp'}, dimensions={1}, use_global_device_ids=true | all-gather | bytes 557056 | tf_op jit(solution)/shard_map/while/body/eval_jaxpr/all_gather | solution.py:126
  263.7 38.5 %all_gather.43 = bf16[64,4096]{1,0:T(8,128)(2,1)S(1)} all-gather(bf16[64,256]{1,0:T(8,128)(2,1)S(1)} %get-tuple-element.885), channel_id=1, replica_groups=mesh['section'=2,'dp'=16] {'dp'}, dimensions={1}, use_global_device_ids=true | all-gather | bytes 557056 | tf_op jit(solution)/shard_map/while/body/eval_jaxpr/all_gather | solution.py:127
  309.2 40.4 %all_gather.42 = bf16[64,4096]{1,0:T(8,128)(2,1)S(1)} all-gather(bf16[64,256]{1,0:T(8,128)(2,1)S(1)} %get-tuple-element.883), channel_id=1, replica_groups=mesh['section'=2,'dp'=16] {'dp'}, dimensions={1}, use_global_device_ids=true | all-gather | bytes 557056 | tf_op jit(solution)/shard_map/while/body/eval_jaxpr/all_gather | solution.py:126
  353.9 38.6 %all_gather.43 = bf16[64,4096]{1,0:T(8,128)(2,1)S(1)} all-gather(bf16[64,256]{1,0:T(8,128)(2,1)S(1)} %get-tuple-element.885), channel_id=1, replica_groups=mesh['section'=2,'dp'=16] {'dp'}, dimensions={1}, use_global_device_ids=true | all-gather | bytes 557056 | tf_op jit(solution)/shard_map/while/body/eval_jaxpr/all_gather | solution.py:127
  403.8 434.3 %while.43 = (s32[]{:T(128)}, bf16[2,64,256]{2,1,0:T(8,128)(2,1)S(1)}, bf16[2,2,64,256]{3,2,1,0:T(8,128)(2,1)S(1)}, f32[2,256,4096]{2,1,0:T(8,128)}, pred[]{:T(51...) while((s32[]{:T(128)}, ...), condition=%wide.region_9.10_spmd, body=%wide.region_4.9_spmd.sunk | while | flops 541523968 | bytes 31794500 | solution.py:219
  404.5 40.6 %all_gather.44 = bf16[64,4096]{1,0:T(8,128)(2,1)S(1)} all-gather(bf16[64,256]{1,0:T(8,128)(2,1)S(1)} %get-tuple-element.906), channel_id=1, replica_groups=mesh['section'=2,'dp'=16] {'dp'}, dimensions={1}, use_global_device_ids=true | all-gather | bytes 557056 | tf_op jit(solution)/shard_map/while/body/eval_jaxpr/all_gather | solution.py:171
  445.1 38.6 %all_gather.45 = bf16[64,4096]{1,0:T(8,128)(2,1)S(1)} all-gather(bf16[64,256]{1,0:T(8,128)(2,1)S(1)} %get-tuple-element.909), channel_id=1, replica_groups=mesh['section'=2,'dp'=16] {'dp'}, dimensions={1}, use_global_device_ids=true | all-gather | bytes 557056 | tf_op jit(solution)/shard_map/while/body/eval_jaxpr/all_gather | solution.py:172
  491.7 39.4 %all-reduce.2 = (f32[64]{0:T(128)S(1)}, f32[64]{0:T(128)}) all-reduce(f32[64]{0:T(128)} %get-tuple-element.910, f32[64]{0:T(128)} %get-tuple-element.911), channel_id=1, replica_groups=mesh['section'=2,'dp'=16] {'dp'}, use_global_device_ids=true, to_apply=%region_8.8 | all-reduce | flops 128 | bytes 1024 | tf_op jit(solution)/shard_map/while/body/eval_jaxpr/psum | solution.py:68
  544.2 5.0 fusion.102
  550.0 38.6 %all_gather.44 = bf16[64,4096]{1,0:T(8,128)(2,1)S(1)} all-gather(bf16[64,256]{1,0:T(8,128)(2,1)S(1)} %get-tuple-element.906), channel_id=1, replica_groups=mesh['section'=2,'dp'=16] {'dp'}, dimensions={1}, use_global_device_ids=true | all-gather | bytes 557056 | tf_op jit(solution)/shard_map/while/body/eval_jaxpr/all_gather | solution.py:171
  588.6 40.7 %all_gather.45 = bf16[64,4096]{1,0:T(8,128)(2,1)S(1)} all-gather(bf16[64,256]{1,0:T(8,128)(2,1)S(1)} %get-tuple-element.909), channel_id=1, replica_groups=mesh['section'=2,'dp'=16] {'dp'}, dimensions={1}, use_global_device_ids=true | all-gather | bytes 557056 | tf_op jit(solution)/shard_map/while/body/eval_jaxpr/all_gather | solution.py:172
  637.3 37.3 %all-reduce.2 = (f32[64]{0:T(128)S(1)}, f32[64]{0:T(128)}) all-reduce(f32[64]{0:T(128)} %get-tuple-element.910, f32[64]{0:T(128)} %get-tuple-element.911), channel_id=1, replica_groups=mesh['section'=2,'dp'=16] {'dp'}, use_global_device_ids=true, to_apply=%region_8.8 | all-reduce | flops 128 | bytes 1024 | tf_op jit(solution)/shard_map/while/body/eval_jaxpr/psum | solution.py:68
  687.8 5.0 fusion.102
  693.5 40.6 %all_gather.44 = bf16[64,4096]{1,0:T(8,128)(2,1)S(1)} all-gather(bf16[64,256]{1,0:T(8,128)(2,1)S(1)} %get-tuple-element.906), channel_id=1, replica_groups=mesh['section'=2,'dp'=16] {'dp'}, dimensions={1}, use_global_device_ids=true | all-gather | bytes 557056 | tf_op jit(solution)/shard_map/while/body/eval_jaxpr/all_gather | solution.py:171
  734.1 38.7 %all_gather.45 = bf16[64,4096]{1,0:T(8,128)(2,1)S(1)} all-gather(bf16[64,256]{1,0:T(8,128)(2,1)S(1)} %get-tuple-element.909), channel_id=1, replica_groups=mesh['section'=2,'dp'=16] {'dp'}, dimensions={1}, use_global_device_ids=true | all-gather | bytes 557056 | tf_op jit(solution)/shard_map/while/body/eval_jaxpr/all_gather | solution.py:172
  780.9 39.0 %all-reduce.2 = (f32[64]{0:T(128)S(1)}, f32[64]{0:T(128)}) all-reduce(f32[64]{0:T(128)} %get-tuple-element.910, f32[64]{0:T(128)} %get-tuple-element.911), channel_id=1, replica_groups=mesh['section'=2,'dp'=16] {'dp'}, use_global_device_ids=true, to_apply=%region_8.8 | all-reduce | flops 128 | bytes 1024 | tf_op jit(solution)/shard_map/while/body/eval_jaxpr/psum | solution.py:68
  828.1 5.0 fusion.101
  833.1 5.0 fusion.102
  (177 shorter events, 130.1 us)
Async XLA Ops:
  4.7 4.5 collective-permute-start.4
  19.6 88.6 %all-to-all-start = ((bf16[2,256,16,256]{3,1,0,2:T(8,128)(2,1)}), bf16[2,256,16,256]{3,1,0,2:T(8,128)(2,1)}, u32[]{:S(2)}, u32[]{:S(2)}) async-start(bf16[2,256,16,256]{3,1,0,2:T(8,128)(2,1)} %copy.11), calls=%async_computation | async-start | bytes 8388608 | tf_op jit(solution)/shard_map/all_to_all | solution.py:104
  30.8 82.3 %copy-start.2 = (bf16[2,2,64,256]{3,2,1,0:T(8,128)(2,1)S(1)}, bf16[2,2,64,256]{3,2,1,0:T(8,128)(2,1)}, u32[]{:S(2)}) copy-start(bf16[2,2,64,256]{3,2,1,0:T(8,128)(2,1)} %param.11) | copy-start | bytes 393220
  172.0 45.6 %collective-permute-start.1 = (bf16[64,256]{1,0:T(8,128)(2,1)}, bf16[64,256]{1,0:T(8,128)(2,1)S(1)}, u32[]{:S(2)}, u32[]{:S(2)}) collective-permute-start(bf16[64,256]{1,0:T(8,128)(2,1)} %get-tuple-element.887), channel_id=1, source_target_pairs={{0,16},{1,17},{2,18},{3,19},{4,20},{5,21},{6,22},{7,23},{8,24},{9,... | collective-permute-start | bytes 98312 | tf_op jit(solution)/shard_map/while/body/eval_jaxpr/ppermute | solution.py:20
  215.3 3.4 collective-permute-start
  262.4 45.6 %collective-permute-start.1 = (bf16[64,256]{1,0:T(8,128)(2,1)}, bf16[64,256]{1,0:T(8,128)(2,1)S(1)}, u32[]{:S(2)}, u32[]{:S(2)}) collective-permute-start(bf16[64,256]{1,0:T(8,128)(2,1)} %get-tuple-element.887), channel_id=1, source_target_pairs={{0,16},{1,17},{2,18},{3,19},{4,20},{5,21},{6,22},{7,23},{8,24},{9,... | collective-permute-start | bytes 98312 | tf_op jit(solution)/shard_map/while/body/eval_jaxpr/ppermute | solution.py:20
  305.7 3.4 collective-permute-start
  352.6 45.7 %collective-permute-start.1 = (bf16[64,256]{1,0:T(8,128)(2,1)}, bf16[64,256]{1,0:T(8,128)(2,1)S(1)}, u32[]{:S(2)}, u32[]{:S(2)}) collective-permute-start(bf16[64,256]{1,0:T(8,128)(2,1)} %get-tuple-element.887), channel_id=1, source_target_pairs={{0,16},{1,17},{2,18},{3,19},{4,20},{5,21},{6,22},{7,23},{8,24},{9,... | collective-permute-start | bytes 98312 | tf_op jit(solution)/shard_map/while/body/eval_jaxpr/ppermute | solution.py:20
  396.1 3.4 collective-permute-start
  485.7 45.3 %copy-start.5 = (f32[64]{0:T(128)S(1)}, f32[64]{0:T(128)}, u32[]{:S(2)}) copy-start(f32[64]{0:T(128)} %get-tuple-element.915) | copy-start | bytes 772 | tf_op jit(solution)/shard_map/while
  532.6 16.7 %collective-permute-start.3 = (bf16[64,256]{1,0:T(8,128)(2,1)}, bf16[64,256]{1,0:T(8,128)(2,1)S(1)}, u32[]{:S(2)}, u32[]{:S(2)}) collective-permute-start(bf16[64,256]{1,0:T(8,128)(2,1)} %get-tuple-element.921), channel_id=1, source_target_pairs={{16,0},{17,1},{18,2},{19,3},{20,4},{21,5},{22,6},{23,7},{24,8},{25... | collective-permute-start | bytes 98312 | tf_op jit(solution)/shard_map/while/body/eval_jaxpr/ppermute | solution.py:20
  536.2 13.1 %collective-permute-start.2 = (bf16[64,256]{1,0:T(8,128)(2,1)S(1)}, bf16[64,256]{1,0:T(8,128)(2,1)S(1)}, u32[]{:S(2)}, u32[]{:S(2)}) collective-permute-start(bf16[64,256]{1,0:T(8,128)(2,1)S(1)} %get-tuple-element.920), channel_id=1, source_target_pairs={{0,16},{1,17},{2,18},{3,19},{4,20},{5,21},{6,22},{7,23},{8,24},{9,... | collective-permute-start | bytes 98312 | tf_op jit(solution)/shard_map/while/body/eval_jaxpr/ppermute | solution.py:20
  544.2 5.1 copy-start.4
  631.4 43.2 %copy-start.5 = (f32[64]{0:T(128)S(1)}, f32[64]{0:T(128)}, u32[]{:S(2)}) copy-start(f32[64]{0:T(128)} %get-tuple-element.915) | copy-start | bytes 772 | tf_op jit(solution)/shard_map/while
  676.1 16.7 %collective-permute-start.3 = (bf16[64,256]{1,0:T(8,128)(2,1)}, bf16[64,256]{1,0:T(8,128)(2,1)S(1)}, u32[]{:S(2)}, u32[]{:S(2)}) collective-permute-start(bf16[64,256]{1,0:T(8,128)(2,1)} %get-tuple-element.921), channel_id=1, source_target_pairs={{16,0},{17,1},{18,2},{19,3},{20,4},{21,5},{22,6},{23,7},{24,8},{25... | collective-permute-start | bytes 98312 | tf_op jit(solution)/shard_map/while/body/eval_jaxpr/ppermute | solution.py:20
  679.7 13.1 %collective-permute-start.2 = (bf16[64,256]{1,0:T(8,128)(2,1)S(1)}, bf16[64,256]{1,0:T(8,128)(2,1)S(1)}, u32[]{:S(2)}, u32[]{:S(2)}) collective-permute-start(bf16[64,256]{1,0:T(8,128)(2,1)S(1)} %get-tuple-element.920), channel_id=1, source_target_pairs={{0,16},{1,17},{2,18},{3,19},{4,20},{5,21},{6,22},{7,23},{8,24},{9,... | collective-permute-start | bytes 98312 | tf_op jit(solution)/shard_map/while/body/eval_jaxpr/ppermute | solution.py:20
  687.8 5.1 copy-start.1
  687.8 5.1 copy-start.4
  774.9 45.0 %copy-start.5 = (f32[64]{0:T(128)S(1)}, f32[64]{0:T(128)}, u32[]{:S(2)}) copy-start(f32[64]{0:T(128)} %get-tuple-element.915) | copy-start | bytes 772 | tf_op jit(solution)/shard_map/while
  821.4 16.7 %collective-permute-start.3 = (bf16[64,256]{1,0:T(8,128)(2,1)}, bf16[64,256]{1,0:T(8,128)(2,1)S(1)}, u32[]{:S(2)}, u32[]{:S(2)}) collective-permute-start(bf16[64,256]{1,0:T(8,128)(2,1)} %get-tuple-element.921), channel_id=1, source_target_pairs={{16,0},{17,1},{18,2},{19,3},{20,4},{21,5},{22,6},{23,7},{24,8},{25... | collective-permute-start | bytes 98312 | tf_op jit(solution)/shard_map/while/body/eval_jaxpr/ppermute | solution.py:20
  825.0 13.1 %collective-permute-start.2 = (bf16[64,256]{1,0:T(8,128)(2,1)S(1)}, bf16[64,256]{1,0:T(8,128)(2,1)S(1)}, u32[]{:S(2)}, u32[]{:S(2)}) collective-permute-start(bf16[64,256]{1,0:T(8,128)(2,1)S(1)} %get-tuple-element.920), channel_id=1, source_target_pairs={{0,16},{1,17},{2,18},{3,19},{4,20},{5,21},{6,22},{7,23},{8,24},{9,... | collective-permute-start | bytes 98312 | tf_op jit(solution)/shard_map/while/body/eval_jaxpr/ppermute | solution.py:20
  833.1 5.1 copy-start.1
  833.1 5.1 copy-start.4
  840.6 4.2 collective-permute-start.5
  (8 other events, 17.1 us)
where the time goes:
time: 852 us; the launch traced here: 850 us
  blocking collectives  606 us (71%)
  waiting for transfers between devices  88.3 us (10%)
  matrix products  64.4 us (8%)
  local copies, waits for them, and re-layouts  37.1 us (4%)
  starting transfers between devices  29.8 us (3%)
  other arithmetic  22.7 us (3%)
    all_gather x3, blocking collectives, forward_tick(): lax.all_gather(for_sending(inputs_now[0]), 'dp', axis=1, tiled=True)  137 us
    all_gather x3, blocking collectives, backward_tick(): lax.all_gather(for_sending(slopes_now[0]), 'dp', axis=1, tiled=True)  120 us
    all_gather x3, blocking collectives, backward_tick(): lax.all_gather(for_sending(slopes_now[1]), 'dp', axis=1, tiled=True)  118 us
    psum x3, blocking collectives, row_totals(): return lax.psum((first_part, second_part), 'dp')  116 us
    all_gather x3, blocking collectives, forward_tick(): lax.all_gather(for_sending(inputs_now[1]), 'dp', axis=1, tiled=True)  116 us
    all_to_all x1, waiting for transfers between devices, body(): lax.all_to_all(split_rows, 'dp', split_axis=2, concat_axis=1, tiled=True)  77.4 us
    dot_general x6, matrix products, backward_tick(): lax.dot_general(normed_locals[stream], slope_fulls[stream], (((0,), (0,))...  30.1 us
    ppermute x12, starting transfers between devices, from_behind(): lax.ppermute(value, axis, [(source, source + steps) for source in range(f...  21 us
  transfers between devices with their start and end apart: 15, of which 6 were waited for; matrix products, arithmetic and copies ran while one was open for 6% of the time, Pallas kernels for 0%

commit v1 on v0

--- a/solution.py
+++ b/solution.py
@@ -1,6 +1,8 @@
 import jax
 import jax.numpy as jnp
 from jax import lax
+from jax.experimental import pallas as pl
+from jax.experimental.pallas import tpu as pltpu
 from jax.sharding import PartitionSpec as P
 
 NORM_EPS = 1e-05
@@ -230,10 +232,335 @@
     )
 
 
+MESH = pl.DeviceIdType.MESH
+F32 = jnp.float32
+BF16 = jnp.bfloat16
+Z_ORDER = (1, 3, 2, 0)
+
+
+def row_sums(values):
+    ones = jnp.ones((8, values.shape[1]), F32)
+    return lax.dot_general(
+        ones,
+        values,
+        (((1,), (1,)), ((), ())),
+        precision=lax.Precision.HIGHEST,
+        preferred_element_type=F32,
+    )
+
+
+def window_kernel(
+    h0, cot, w_hbm, ad, au, gd, gu, wg_hbm,
+    w, gf, part, a1, b1, a2, b2, sa, sb, tz, zra, zrb, stats, back, hid, nrm, nrm_t, own, wg,
+    w_sem, wg_sem, st_s, st_r, ag_s, ag_r, own_s, rs_s, rs_r, z_s, za_r, zb_r, ex_s, ex_r,
+):
+    tok, cols = h0.shape
+    half = tok // 2
+    low, high = pl.ds(0, half), pl.ds(half, half)
+    width = cols * 16
+    sec = lax.axis_index("section")
+    dp = lax.axis_index("dp")
+    z, y, x = dp // 4, (dp // 2) % 2, dp % 2
+    px, py = dp + 1 - 2 * x, dp + 2 - 4 * y
+
+    def zp(dz):
+        return ((z + dz) % 4) * 4 + y * 2 + x
+
+    def block_cols(dz, ry, rx):
+        yy = 1 - y if ry else y
+        xx = 1 - x if rx else x
+        return pl.ds(pl.multiple_of((((z + dz) % 4) * 4 + yy * 2 + xx) * cols, cols), cols)
+
+    def send(src, dst, s_sem, r_sem, section, chip):
+        copy = pltpu.make_async_remote_copy(
+            src_ref=src, dst_ref=dst, send_sem=s_sem, recv_sem=r_sem,
+            device_id=(section, chip), device_id_type=MESH,
+        )
+        copy.start()
+        return copy
+
+    def arrived(dst, r_sem):
+        pltpu.make_async_remote_copy(
+            src_ref=dst, dst_ref=dst, send_sem=r_sem, recv_sem=r_sem,
+            device_id=(sec, dp), device_id_type=MESH,
+        ).wait_recv()
+
+    load_w = pltpu.make_async_copy(w_hbm.at[0], w, w_sem)
+    load_w.start()
+
+    barrier = pltpu.get_barrier_semaphore()
+    for step in range(1, 16):
+        pl.semaphore_signal(barrier, inc=1, device_id=(sec, (dp + step) % 16), device_id_type=MESH)
+    for chip in (dp, px, py, zp(1), zp(2), zp(3)):
+        pl.semaphore_signal(barrier, inc=1, device_id=(1 - sec, chip), device_id_type=MESH)
+    pl.semaphore_wait(barrier, 21)
+
+    def stat_send(k, value):
+        stats[k, dp] = value
+        copies = []
+        for step in range(1, 16):
+            copies.append(send(
+                stats.at[k, dp], stats.at[k, dp], st_s.at[k, step], st_r.at[k, step],
+                sec, (dp + step) % 16,
+            ))
+        return copies
+
+    def stat_total(k):
+        for step in range(1, 16):
+            arrived(stats.at[k, (dp + 16 - step) % 16], st_r.at[k, step])
+        total = jnp.sum(stats[k], axis=0)
+        return jnp.transpose(total)
+
+    def gather_own(src, section, include_self):
+        copies = []
+        for dz in (1, 2, 3):
+            copies.append(send(src, gf.at[4 - dz, 0, 0], own_s.at[dz], ag_r.at[4 - dz, 0], section, zp(dz)))
+        copies.append(send(src, gf.at[0, 0, 1], own_s.at[4], ag_r.at[0, 1], section, px))
+        copies.append(send(src, gf.at[0, 1, 0], own_s.at[5], ag_r.at[0, 2], section, py))
+        if include_self:
+            copies.append(send(src, gf.at[0, 0, 0], own_s.at[0], ag_r.at[0, 0], section, dp))
+        return copies
+
+    def gather_rest(use, own_arrives):
+        copies = []
+        for dz in (1, 3, 2):
+            arrived(gf.at[dz, 0, 0], ag_r.at[dz, 0])
+            copies.append(send(gf.at[dz, 0, 0], gf.at[dz, 0, 1], ag_s.at[dz, 0], ag_r.at[dz, 1], sec, px))
+            copies.append(send(gf.at[dz, 0, 0], gf.at[dz, 1, 0], ag_s.at[dz, 1], ag_r.at[dz, 2], sec, py))
+            if dz == 1:
+                if own_arrives:
+                    arrived(gf.at[0, 0, 0], ag_r.at[0, 0])
+                use(0, 0, 0)
+            use(dz, 0, 0)
+        for dz in (0, 1, 3, 2):
+            arrived(gf.at[dz, 0, 1], ag_r.at[dz, 1])
+            copies.append(send(
+                gf.at[dz, 0, 1, low], gf.at[dz, 1, 1, low], ag_s.at[dz, 2], ag_r.at[dz, 3], sec, py))
+            arrived(gf.at[dz, 1, 0], ag_r.at[dz, 2])
+            copies.append(send(
+                gf.at[dz, 1, 0, high], gf.at[dz, 1, 1, high], ag_s.at[dz, 3], ag_r.at[dz, 4], sec, px))
+            use(dz, 0, 1)
+            use(dz, 1, 0)
+        for dz in (0, 1, 3, 2):
+            arrived(gf.at[dz, 1, 1, low], ag_r.at[dz, 3])
+            arrived(gf.at[dz, 1, 1, high], ag_r.at[dz, 4])
+            use(dz, 1, 1)
+        return copies
+
+    def scatter_first(rows):
+        copies = []
+        for dz in Z_ORDER:
+            for ry, rx in ((0, 1), (1, 1), (1, 0), (0, 0)):
+                part[dz, ry, rx] = jnp.dot(
+                    rows[...], w[:, block_cols(dz, ry, rx)], preferred_element_type=F32
+                ).astype(BF16)
+                if (ry, rx) == (1, 1):
+                    copies.append(send(
+                        part.at[dz, pl.ds(0, 2), 1, low], a1.at[dz], rs_s.at[dz, 0], rs_r.at[dz, 0], sec, px))
+                if (ry, rx) == (1, 0):
+                    copies.append(send(
+                        part.at[dz, 1, pl.ds(0, 2), high], b1.at[dz], rs_s.at[dz, 1], rs_r.at[dz, 1], sec, py))
+        return copies
+
+    def scatter_second():
+        copies = []
+        for dz in Z_ORDER:
+            arrived(a1.at[dz], rs_r.at[dz, 0])
+            sa[dz] = (part[dz, 1, 0, low].astype(F32) + a1[dz, 1].astype(F32)).astype(BF16)
+            copies.append(send(sa.at[dz], a2.at[dz], rs_s.at[dz, 2], rs_r.at[dz, 2], sec, py))
+            arrived(b1.at[dz], rs_r.at[dz, 1])
+            sb[dz] = (part[dz, 0, 1, high].astype(F32) + b1[dz, 1].astype(F32)).astype(BF16)
+            copies.append(send(sb.at[dz], b2.at[dz], rs_s.at[dz, 3], rs_r.at[dz, 3], sec, px))
+        return copies
+
+    def scatter_third(landing, r_sems, self_too):
+        copies = []
+        for dz in Z_ORDER:
+            arrived(a2.at[dz], rs_r.at[dz, 2])
+            tz[dz, low] = (
+                part[dz, 0, 0, low].astype(F32) + a1[dz, 0].astype(F32) + a2[dz].astype(F32)
+            ).astype(BF16)
+            arrived(b2.at[dz], rs_r.at[dz, 3])
+            tz[dz, high] = (
+                part[dz, 0, 0, high].astype(F32) + b1[dz, 0].astype(F32) + b2[dz].astype(F32)
+            ).astype(BF16)
+            if dz:
+                copies.append(send(tz.at[dz], landing.at[4 - dz], z_s.at[dz], r_sems.at[4 - dz], 1, zp(dz)))
+            elif self_too:
+                copies.append(send(tz.at[0], landing.at[0], z_s.at[0], r_sems.at[0], 1, dp))
+        return copies
+
+    def back_step(dz, ry, rx):
+        return lax.dot_general(
+            gf[dz, ry, rx], w[:, block_cols(dz, ry, rx)], (((1,), (1,)), ((), ())),
+            preferred_element_type=F32,
+        )
+
+    def weight_step(dz, ry, rx):
+        spot = block_cols(dz, ry, rx)
+        wg[dz * 4 + ry * 2 + rx] = jnp.dot(nrm_t[...], gf[dz, ry, rx], preferred_element_type=F32)
+        copy = pltpu.make_async_copy(
+            wg.at[dz * 4 + ry * 2 + rx], wg_hbm.at[:, spot], wg_sem.at[dz * 4 + ry * 2 + rx])
+        copy.start()
+        return copy
+
+    def scale_of(totals):
+        return lax.rsqrt(totals[:, 0:1] / width + NORM_EPS)
+
+    def set_normed(values, scale):
+        normed = values.astype(F32) * scale
+        nrm[...] = normed.astype(BF16)
+        nrm_t[...] = jnp.transpose(normed).astype(BF16)
+
+    entered = h0[...].astype(F32)
+
+    @pl.when(sec == 0)
+    def _():
+        copies = stat_send(0, row_sums(entered * entered))
+        load_w.wait()
+        copies += scatter_first(h0)
+        copies += scatter_second()
+        copies += scatter_third(zra, za_r, True)
+        scale = scale_of(stat_total(0))
+        set_normed(h0[...], scale)
+        back[...] = jnp.zeros_like(back)
+        writes = []
+
+        def use(dz, ry, rx):
+            back[...] += back_step(dz, ry, rx)
+            writes.append(weight_step(dz, ry, rx))
+
+        copies += gather_rest(use, True)
+        normed = nrm[...].astype(F32)
+        copies += stat_send(2, row_sums(back[...] * normed))
+        gu[...] = gf[0, 0, 0, high]
+        arrived(ad, ex_r.at[0])
+        dot = stat_total(2)[:, 0:1]
+        own[...] = (
+            gf[0, 0, 0].astype(F32) + scale * (back[...] - normed * dot / width)
+        ).astype(BF16)
+        copies.append(send(own.at[high], gu, ex_s.at[0], ex_r.at[1], 1, dp))
+        gd[...] = own[low]
+        arrived(au, ex_r.at[2])
+        for copy in writes:
+            copy.wait()
+        for copy in copies:
+            copy.wait_send()
+
+    @pl.when(sec == 1)
+    def _():
+        copies = stat_send(0, row_sums(entered * entered))
+        copies += gather_own(cot, 1, False)
+        gf[0, 0, 0] = cot[...]
+        back[...] = jnp.zeros_like(back)
+        load_w.wait()
+
+        def use(dz, ry, rx):
+            back[...] += back_step(dz, ry, rx)
+
+        copies += gather_rest(use, False)
+        for copy in copies:
+            copy.wait_send()
+        scale = scale_of(stat_total(0))
+        for dz in (0, 1, 3, 2):
+            arrived(zra.at[dz], za_r.at[dz])
+        mixed = (
+            zra[0].astype(F32) + zra[1].astype(F32) + zra[2].astype(F32) + zra[3].astype(F32)
+        )
+        hid[...] = (entered + scale * mixed).astype(BF16)
+        hidden = hid[...].astype(F32)
+        first = lax.broadcasted_iota(jnp.int32, (8, tok), 0) == 0
+        copies = stat_send(1, jnp.where(first, row_sums(hidden * hidden), row_sums(back[...] * hidden)))
+        copies += scatter_first(hid)
+        copies.append(send(hid.at[low], ad, ex_s.at[0], ex_r.at[0], 0, dp))
+        au[...] = hid[high]
+        totals = stat_total(1)
+        scale = scale_of(totals)
+        dot = totals[:, 1:2] * scale
+        set_normed(hid[...], scale)
+        own[...] = (
+            cot[...].astype(F32) + scale * (back[...] - nrm[...].astype(F32) * dot / width)
+        ).astype(BF16)
+        copies += gather_own(own, 0, True)
+        copies += scatter_second()
+        gd[...] = own[low]
+        copies += scatter_third(zrb, zb_r, False)
+        writes = []
+        for dz in range(4):
+            for ry in range(2):
+                for rx in range(2):
+                    writes.append(weight_step(dz, ry, rx))
+        mixed = tz[0].astype(F32)
+        for dz in (1, 2, 3):
+            arrived(zrb.at[dz], zb_r.at[dz])
+            mixed = mixed + zrb[dz].astype(F32)
+        tz[0] = (hid[...].astype(F32) + scale * mixed).astype(BF16)
+        copies.append(send(tz.at[0, high], au, ex_s.at[1], ex_r.at[2], 0, dp))
+        ad[...] = tz[0, low]
+        arrived(gu, ex_r.at[1])
+        for copy in writes:
+            copy.wait()
+        for copy in copies:
+            copy.wait_send()
+
+
+def direct_body(entering, cotangent, weights):
+    streams, micro, tok_mb, cols = entering.shape
+    tok = streams * micro * tok_mb
+    half = tok // 2
+    width = weights.shape[2]
+    rows = entering.reshape(tok, cols)
+    slopes = cotangent.reshape(tok, cols)
+    vm = pl.BlockSpec(memory_space=pltpu.VMEM)
+    hbm = pl.BlockSpec(memory_space=pl.ANY)
+    half_out = jax.ShapeDtypeStruct((half, cols), BF16)
+    dma = pltpu.SemaphoreType.DMA
+    ad, au, gd, gu, wg = pl.pallas_call(
+        window_kernel,
+        out_shape=(half_out,) * 4 + (jax.ShapeDtypeStruct((cols, width), F32),),
+        in_specs=[vm, vm, hbm],
+        out_specs=(vm,) * 4 + (hbm,),
+        scratch_shapes=[
+            pltpu.VMEM((cols, width), BF16),
+            pltpu.VMEM((4, 2, 2, tok, cols), BF16),
+            pltpu.VMEM((4, 2, 2, tok, cols), BF16),
+            pltpu.VMEM((4, 2, half, cols), BF16),
+            pltpu.VMEM((4, 2, half, cols), BF16),
+            pltpu.VMEM((4, half, cols), BF16),
+            pltpu.VMEM((4, half, cols), BF16),
+            pltpu.VMEM((4, half, cols), BF16),
+            pltpu.VMEM((4, half, cols), BF16),
+            pltpu.VMEM((4, tok, cols), BF16),
+            pltpu.VMEM((4, tok, cols), BF16),
+            pltpu.VMEM((4, tok, cols), BF16),
+            pltpu.VMEM((3, 16, 8, tok), F32),
+            pltpu.VMEM((tok, cols), F32),
+            pltpu.VMEM((tok, cols), BF16),
+            pltpu.VMEM((tok, cols), BF16),
+            pltpu.VMEM((cols, tok), BF16),
+            pltpu.VMEM((tok, cols), BF16),
+            pltpu.VMEM((16, cols, cols), F32),
+            dma, dma((16,)), dma((3, 16)), dma((3, 16)),
+            dma((4, 4)), dma((4, 5)), dma((6,)),
+            dma((4, 4)), dma((4, 4)), dma((4,)), dma((4,)), dma((4,)),
+            dma((2,)), dma((3,)),
+        ],
+        compiler_params=pltpu.CompilerParams(
+            collective_id=0, has_side_effects=True, vmem_limit_bytes=48 * 1024 * 1024
+        ),
+        cost_estimate=pl.CostEstimate(
+            flops=6 * tok * cols * width, bytes_accessed=6 * cols * width, transcendentals=2 * tok
+        ),
+    )(rows, slopes, weights)
+    shape = (1, micro, tok_mb, cols)
+    return (ad.reshape(shape), au.reshape(shape), gd.reshape(shape), gu.reshape(shape), wg[None])
+
+
 def solution(mesh):
     placed = (P(None, None, None, "dp"), P(None, None, None, "dp"), P("section", "dp", None))
+    exact = dict(mesh.shape) == {"section": 2, "dp": 16}
     return jax.shard_map(
-        body,
+        direct_body if exact else body,
         mesh=mesh,
         in_specs=placed,
         out_specs=(

time: 852 us -> 69.4 us (0.08)
  blocking collectives: 606 us -> 0 us
  waiting for transfers between devices: 88.3 us -> 0 us
  matrix products: 64.4 us -> 0 us
  Pallas kernels: 0 us -> 57.9 us
  starting transfers between devices: 29.8 us -> 0 us
  local copies, waits for them, and re-layouts: 37.1 us -> 10.6 us
  other arithmetic: 22.7 us -> 0 us
    all_gather x12 -> x0, blocking collectives: 490 us -> none  [the longest x3 137 us: forward_tick(): lax.all_gather(for_sending(inputs_now[0]), 'dp', axis=1, tiled=True)]
    psum x3 -> x0, blocking collectives: 116 us -> none  [row_totals(): return lax.psum((first_part, second_part), 'dp')]
    all_to_all x1 -> x0, waiting for transfers between devices: 77.4 us -> none  [body(): lax.all_to_all(split_rows, 'dp', split_axis=2, concat_axis=1, tiled=True)]
    dot_general x18 -> x0, matrix products: 64.4 us -> none  [the longest x6 30.1 us: backward_tick(): lax.dot_general(normed_locals[stream], slope_fulls[stream], (((0,), (0,))...]
    pallas_call x0 -> x1, Pallas kernels: none -> 57.9 us  [direct_body(): pl.pallas_call(window_kernel, out_shape=(half_out,) * 4 + (jax.ShapeDtype...]
    ppermute x14 -> x0, starting transfers between devices: 21.5 us -> none  [the longest x12 21 us: from_behind(): lax.ppermute(value, axis, [(source, source + steps) for source in range(f...]
    ppermute x14 -> x0, waiting for transfers between devices: 10.9 us -> none  [the longest x2 7.44 us: swapped_2(): return lax.ppermute(block, axis, route)]
    dynamic_update_slice x12 -> x0, other arithmetic: 10.6 us -> none  [place_slot(): return lax.dynamic_update_slice(store, kept[None, None], starts)]
  transfers between devices with their start and end apart: 15 -> 0, of which waited for: 6 -> 0; matrix products, arithmetic and copies ran while one was open for 6% -> 0% of each run, Pallas kernels for 0% -> 0%
where the time goes in v1:
time: 69.4 us; the launch traced here: 69.2 us
  Pallas kernels  57.9 us (83%)
  local copies, waits for them, and re-layouts  10.6 us (15%)
    pallas_call x1, Pallas kernels, direct_body(): pl.pallas_call(window_kernel, out_shape=(half_out,) * 4 + (jax.ShapeDtype...  57.9 us
    unnamed x11, local copies, waits for them, and re-layouts  10.6 us

profile of v1, /device:TPU:0, one launch (start us, length us, event | category | flops | bytes accessed | tf_op | source)
XLA Modules:
  0.0 69.2 jit_solution(8838868487299336977)
XLA Ops:
  0.6 0.0 copy-start
  0.6 1.6 %copy-done = bf16[1,256,4096]{2,1,0:T(8,128)(2,1)S(1)} copy-done((bf16[1,256,4096]{2,1,0:T(8,128)(2,1)S(1)}, bf16[1,256,4096]{2,1,0:T(8,128)(2,1)}, u32[]{:S(2)}) %copy-start) | copy-done | bytes 2097176
  2.2 0.0 copy-start.1
  2.2 0.9 %copy-done.1 = bf16[2,2,64,256]{3,2,1,0:T(8,128)(2,1)S(1)} copy-done((bf16[2,2,64,256]{3,2,1,0:T(8,128)(2,1)S(1)}, bf16[2,2,64,256]{3,2,1,0:T(8,128)(2,1)}, u32[]{:S(2)}) %copy-start.1) | copy-done | bytes 131096
  3.1 0.0 copy-start.2
  3.1 0.9 %copy-done.2 = bf16[2,2,64,256]{3,2,1,0:T(8,128)(2,1)S(1)} copy-done((bf16[2,2,64,256]{3,2,1,0:T(8,128)(2,1)S(1)}, bf16[2,2,64,256]{3,2,1,0:T(8,128)(2,1)}, u32[]{:S(2)}) %copy-start.2) | copy-done | bytes 131096
  4.0 57.9 %shard_map.74 = (bf16[128,256]{1,0:T(8,128)(2,1)S(1)}, bf16[128,256]{1,0:T(8,128)(2,1)S(1)}, bf16[128,256]{1,0:T(8,128)(2,1)S(1)}, bf16[128,256]{1,0:T(8,128)(2,1)S(1)}, f32[256,4096]{1,0:T(8,128)}) custom-call(bf16[256,256]{1,0:T(8,128)(2,1)S(1)} %bitcast.11, bf16[256,256]{1,0:T(8,128)(2,1)S(1)} %bitcast.12, bf16[1,256,4096]{2,1,0:T(8,128)(2,1)S(1)} %copy-done), custom_call_target="tpu_custom_call" | custom-call | flops 1610612736 | bytes 6291456 | tf_op jit(solution)/shard_map/pallas_call | solution.py:518
  62.0 0.6 copy.13
  62.6 0.6 copy.14
  63.2 0.6 copy.15
  63.9 0.6 copy.16
  64.5 4.7 %copy.17 = f32[1,256,4096]{2,1,0:T(8,128)} copy(f32[1,256,4096]{2,1,0:T(8,128)} %bitcast.13) | data formatting | bytes 8388608
Async XLA Ops:
  0.6 1.6 %copy-start = (bf16[1,256,4096]{2,1,0:T(8,128)(2,1)S(1)}, bf16[1,256,4096]{2,1,0:T(8,128)(2,1)}, u32[]{:S(2)}) copy-start(bf16[1,256,4096]{2,1,0:T(8,128)(2,1)} %w_hbm.1) | copy-start | bytes 6291460
  2.2 0.9 %copy-start.1 = (bf16[2,2,64,256]{3,2,1,0:T(8,128)(2,1)S(1)}, bf16[2,2,64,256]{3,2,1,0:T(8,128)(2,1)}, u32[]{:S(2)}) copy-start(bf16[2,2,64,256]{3,2,1,0:T(8,128)(2,1)} %param.3) | copy-start | bytes 393220
  3.1 0.9 %copy-start.2 = (bf16[2,2,64,256]{3,2,1,0:T(8,128)(2,1)S(1)}, bf16[2,2,64,256]{3,2,1,0:T(8,128)(2,1)}, u32[]{:S(2)}) copy-start(bf16[2,2,64,256]{3,2,1,0:T(8,128)(2,1)} %param.4) | copy-start | bytes 393220

commit v2 on v1

--- a/solution.py
+++ b/solution.py
@@ -250,9 +250,9 @@
 
 
 def window_kernel(
-    h0, cot, w_hbm, ad, au, gd, gu, wg_hbm,
-    w, gf, part, a1, b1, a2, b2, sa, sb, tz, zra, zrb, stats, back, hid, nrm, nrm_t, own, wg,
-    w_sem, wg_sem, st_s, st_r, ag_s, ag_r, own_s, rs_s, rs_r, z_s, za_r, zb_r, ex_s, ex_r,
+    h0_hbm, cot_hbm, w_hbm, ad, au, gd, gu, nrm_t, gf_hbm,
+    h0, cot, w, gf, part, a1, b1, a2, b2, sa, sb, tz, zra, zrb, stats, back, hid, nrm, own,
+    in_sem, keep_sem, st_s, st_r, ag_s, ag_r, own_s, rs_s, rs_r, z_s, za_r, zb_r, ex_s, ex_r,
 ):
     tok, cols = h0.shape
     half = tok // 2
@@ -285,7 +285,11 @@
             device_id=(sec, dp), device_id_type=MESH,
         ).wait_recv()
 
-    load_w = pltpu.make_async_copy(w_hbm.at[0], w, w_sem)
+    load_h = pltpu.make_async_copy(h0_hbm, h0, in_sem.at[0])
+    load_h.start()
+    load_c = pltpu.make_async_copy(cot_hbm, cot, in_sem.at[1])
+    load_c.start()
+    load_w = pltpu.make_async_copy(w_hbm.at[0], w, in_sem.at[2])
     load_w.start()
 
     barrier = pltpu.get_barrier_semaphore()
@@ -296,7 +300,7 @@
     pl.semaphore_wait(barrier, 21)
 
     def stat_send(k, value):
-        stats[k, dp] = value
+        stats[k, dp] = value[0:2]
         copies = []
         for step in range(1, 16):
             copies.append(send(
@@ -309,7 +313,7 @@
         for step in range(1, 16):
             arrived(stats.at[k, (dp + 16 - step) % 16], st_r.at[k, step])
         total = jnp.sum(stats[k], axis=0)
-        return jnp.transpose(total)
+        return jnp.transpose(jnp.concatenate([total] * 4, axis=0))
 
     def gather_own(src, section, include_self):
         copies = []
@@ -347,9 +351,9 @@
             use(dz, 1, 1)
         return copies
 
-    def scatter_first(rows):
+    def scatter_first(rows, order):
         copies = []
-        for dz in Z_ORDER:
+        for dz in order:
             for ry, rx in ((0, 1), (1, 1), (1, 0), (0, 0)):
                 part[dz, ry, rx] = jnp.dot(
                     rows[...], w[:, block_cols(dz, ry, rx)], preferred_element_type=F32
@@ -396,11 +400,9 @@
             preferred_element_type=F32,
         )
 
-    def weight_step(dz, ry, rx):
-        spot = block_cols(dz, ry, rx)
-        wg[dz * 4 + ry * 2 + rx] = jnp.dot(nrm_t[...], gf[dz, ry, rx], preferred_element_type=F32)
+    def keep(dz, ry, rx):
         copy = pltpu.make_async_copy(
-            wg.at[dz * 4 + ry * 2 + rx], wg_hbm.at[:, spot], wg_sem.at[dz * 4 + ry * 2 + rx])
+            gf.at[dz, ry, rx], gf_hbm.at[dz, ry, rx], keep_sem.at[dz * 4 + ry * 2 + rx])
         copy.start()
         return copy
 
@@ -412,13 +414,14 @@
         nrm[...] = normed.astype(BF16)
         nrm_t[...] = jnp.transpose(normed).astype(BF16)
 
-    entered = h0[...].astype(F32)
-
     @pl.when(sec == 0)
     def _():
+        load_h.wait()
+        entered = h0[...].astype(F32)
         copies = stat_send(0, row_sums(entered * entered))
         load_w.wait()
-        copies += scatter_first(h0)
+        copies += scatter_first(h0, Z_ORDER)
+        load_c.wait()
         copies += scatter_second()
         copies += scatter_third(zra, za_r, True)
         scale = scale_of(stat_total(0))
@@ -428,7 +431,7 @@
 
         def use(dz, ry, rx):
             back[...] += back_step(dz, ry, rx)
-            writes.append(weight_step(dz, ry, rx))
+            writes.append(keep(dz, ry, rx))
 
         copies += gather_rest(use, True)
         normed = nrm[...].astype(F32)
@@ -449,14 +452,20 @@
 
     @pl.when(sec == 1)
     def _():
-        copies = stat_send(0, row_sums(entered * entered))
-        copies += gather_own(cot, 1, False)
+        load_c.wait()
+        copies = gather_own(cot, 1, False)
         gf[0, 0, 0] = cot[...]
+        load_h.wait()
+        entered = h0[...].astype(F32)
+        copies += stat_send(0, row_sums(entered * entered))
         back[...] = jnp.zeros_like(back)
         load_w.wait()
 
+        writes = []
+
         def use(dz, ry, rx):
             back[...] += back_step(dz, ry, rx)
+            writes.append(keep(dz, ry, rx))
 
         copies += gather_rest(use, False)
         for copy in copies:
@@ -471,7 +480,7 @@
         hidden = hid[...].astype(F32)
         first = lax.broadcasted_iota(jnp.int32, (8, tok), 0) == 0
         copies = stat_send(1, jnp.where(first, row_sums(hidden * hidden), row_sums(back[...] * hidden)))
-        copies += scatter_first(hid)
+        copies += scatter_first(hid, Z_ORDER[:2])
         copies.append(send(hid.at[low], ad, ex_s.at[0], ex_r.at[0], 0, dp))
         au[...] = hid[high]
         totals = stat_total(1)
@@ -482,14 +491,10 @@
             cot[...].astype(F32) + scale * (back[...] - nrm[...].astype(F32) * dot / width)
         ).astype(BF16)
         copies += gather_own(own, 0, True)
+        copies += scatter_first(hid, Z_ORDER[2:])
         copies += scatter_second()
         gd[...] = own[low]
         copies += scatter_third(zrb, zb_r, False)
-        writes = []
-        for dz in range(4):
-            for ry in range(2):
-                for rx in range(2):
-                    writes.append(weight_step(dz, ry, rx))
         mixed = tz[0].astype(F32)
         for dz in (1, 2, 3):
             arrived(zrb.at[dz], zb_r.at[dz])
@@ -504,6 +509,33 @@
             copy.wait_send()
 
 
+def finish_kernel(nrm_t, gf_hbm, *refs):
+    kept, outs, (wg_hbm, gf, wg, in_sem, wg_sem, out_sem) = refs[:4], refs[4:8], refs[8:]
+    cols = nrm_t.shape[0]
+    dp = lax.axis_index("dp")
+    z, y, x = dp // 4, (dp // 2) % 2, dp % 2
+    loads, copies = [], []
+    for k in range(16):
+        spot = (k // 4, (k // 2) % 2, k % 2)
+        loads.append(pltpu.make_async_copy(gf_hbm.at[spot], gf.at[k], in_sem.at[k]))
+        loads[k].start()
+    for k in range(4):
+        copies.append(pltpu.make_async_copy(kept[k], outs[k], out_sem.at[k]))
+        copies[k].start()
+    for k in range(16):
+        loads[k].wait()
+        yy = 1 - y if (k // 2) % 2 else y
+        xx = 1 - x if k % 2 else x
+        block = ((z + k // 4) % 4) * 4 + yy * 2 + xx
+        wg[k] = jnp.dot(nrm_t[...], gf[k], preferred_element_type=F32)
+        spot = pl.ds(pl.multiple_of(block * cols, cols), cols)
+        copy = pltpu.make_async_copy(wg.at[k], wg_hbm.at[:, spot], wg_sem.at[k])
+        copy.start()
+        copies.append(copy)
+    for copy in copies:
+        copy.wait()
+
+
 def direct_body(entering, cotangent, weights):
     streams, micro, tok_mb, cols = entering.shape
     tok = streams * micro * tok_mb
@@ -515,12 +547,17 @@
     hbm = pl.BlockSpec(memory_space=pl.ANY)
     half_out = jax.ShapeDtypeStruct((half, cols), BF16)
     dma = pltpu.SemaphoreType.DMA
-    ad, au, gd, gu, wg = pl.pallas_call(
+    *kept, nrm_t, gathered = pl.pallas_call(
         window_kernel,
-        out_shape=(half_out,) * 4 + (jax.ShapeDtypeStruct((cols, width), F32),),
-        in_specs=[vm, vm, hbm],
-        out_specs=(vm,) * 4 + (hbm,),
+        out_shape=(half_out,) * 4 + (
+            jax.ShapeDtypeStruct((cols, tok), BF16),
+            jax.ShapeDtypeStruct((4, 2, 2, tok, cols), BF16),
+        ),
+        in_specs=[hbm, hbm, hbm],
+        out_specs=(vm,) * 5 + (hbm,),
         scratch_shapes=[
+            pltpu.VMEM((tok, cols), BF16),
+            pltpu.VMEM((tok, cols), BF16),
             pltpu.VMEM((cols, width), BF16),
             pltpu.VMEM((4, 2, 2, tok, cols), BF16),
             pltpu.VMEM((4, 2, 2, tok, cols), BF16),
@@ -533,27 +570,40 @@
             pltpu.VMEM((4, tok, cols), BF16),
             pltpu.VMEM((4, tok, cols), BF16),
             pltpu.VMEM((4, tok, cols), BF16),
-            pltpu.VMEM((3, 16, 8, tok), F32),
+            pltpu.VMEM((3, 16, 2, tok), F32),
             pltpu.VMEM((tok, cols), F32),
             pltpu.VMEM((tok, cols), BF16),
             pltpu.VMEM((tok, cols), BF16),
-            pltpu.VMEM((cols, tok), BF16),
             pltpu.VMEM((tok, cols), BF16),
-            pltpu.VMEM((16, cols, cols), F32),
-            dma, dma((16,)), dma((3, 16)), dma((3, 16)),
+            dma((3,)), dma((16,)), dma((3, 16)), dma((3, 16)),
             dma((4, 4)), dma((4, 5)), dma((6,)),
             dma((4, 4)), dma((4, 4)), dma((4,)), dma((4,)), dma((4,)),
             dma((2,)), dma((3,)),
         ],
         compiler_params=pltpu.CompilerParams(
-            collective_id=0, has_side_effects=True, vmem_limit_bytes=48 * 1024 * 1024
+            collective_id=0, has_side_effects=True, vmem_limit_bytes=63 * 1024 * 1024
         ),
         cost_estimate=pl.CostEstimate(
-            flops=6 * tok * cols * width, bytes_accessed=6 * cols * width, transcendentals=2 * tok
+            flops=4 * tok * cols * width, bytes_accessed=4 * cols * width, transcendentals=2 * tok
         ),
     )(rows, slopes, weights)
+    *outs, weight_grad = pl.pallas_call(
+        finish_kernel,
+        out_shape=(half_out,) * 4 + (jax.ShapeDtypeStruct((cols, width), F32),),
+        in_specs=[vm, hbm] + [vm] * 4,
+        out_specs=(hbm,) * 5,
+        scratch_shapes=[
+            pltpu.VMEM((16, tok, cols), BF16),
+            pltpu.VMEM((16, cols, cols), F32),
+            dma((16,)), dma((16,)), dma((4,)),
+        ],
+        compiler_params=pltpu.CompilerParams(vmem_limit_bytes=63 * 1024 * 1024),
+        cost_estimate=pl.CostEstimate(
+            flops=2 * tok * cols * width, bytes_accessed=6 * cols * width, transcendentals=0
+        ),
+    )(nrm_t, gathered, *kept)
     shape = (1, micro, tok_mb, cols)
-    return (ad.reshape(shape), au.reshape(shape), gd.reshape(shape), gu.reshape(shape), wg[None])
+    return (*(out.reshape(shape) for out in outs), weight_grad[None])
 
 
 def solution(mesh):

time: 69.4 us -> 65.3 us (0.941)
  local copies, waits for them, and re-layouts: 10.6 us -> 0 us
  Pallas kernels: 57.9 us -> 64.4 us
    unnamed x11 -> x0, local copies, waits for them, and re-layouts: 10.6 us -> none
    pallas_call x0 -> x1, Pallas kernels: none -> 6.48 us  [direct_body(): pl.pallas_call(finish_kernel, out_shape=(half_out,) * 4 + (jax.ShapeDtype...]
where the time goes in v2:
time: 65.3 us; the launch traced here: 65.1 us
  Pallas kernels  64.4 us (99%)
    pallas_call x1, Pallas kernels, direct_body(): pl.pallas_call(window_kernel, out_shape=(half_out,) * 4 + (jax.ShapeDtype...  58 us
    pallas_call x1, Pallas kernels, direct_body(): pl.pallas_call(finish_kernel, out_shape=(half_out,) * 4 + (jax.ShapeDtype...  6.48 us

profile of v2, /device:TPU:0, one launch (start us, length us, event | category | flops | bytes accessed | tf_op | source)
XLA Modules:
  0.0 65.1 jit_solution(18375608971743837531)
XLA Ops:
  0.6 58.0 %shard_map.74 = (bf16[128,256]{1,0:T(8,128)(2,1)}, bf16[128,256]{1,0:T(8,128)(2,1)}, bf16[128,256]{1,0:T(8,128)(2,1)}, bf16[128,256]{1,0:T(8,128)(2,1)}, bf16[25...) custom-call(bf16[256,256]{1,0:T(8,128)(2,1)} %bitcast.8, bf16[256,256]{1,0:T(8,128)(2,1)} %bitcast.9, ...), custom_call_target="tpu_custom_call" | custom-call | flops 1073741824 | bytes 4194304 | tf_op jit(solution)/shard_map/pallas_call | solution.py:550
  58.6 6.5 %shard_map.75 = (bf16[128,256]{1,0:T(8,128)(2,1)}, bf16[128,256]{1,0:T(8,128)(2,1)}, bf16[128,256]{1,0:T(8,128)(2,1)}, bf16[128,256]{1,0:T(8,128)(2,1)}, f32[256,4096]{1,0:T(8,128)}) custom-call(bf16[256,256]{1,0:T(8,128)(2,1)} %get-tuple-element.16.nrm_t, bf16[4,2,2,256,256]{4,3,2,1,0:T(8,128)(2,1)} %get-tuple-element.17.gf_hbm, ...), custom_call_target="tpu_custom_call" | custom-call | flops 536870912 | bytes 6291456 | tf_op jit(solution)/shard_map/pallas_call | solution.py:590

commit v3 on v2

--- a/solution.py
+++ b/solution.py
@@ -235,7 +235,7 @@
 MESH = pl.DeviceIdType.MESH
 F32 = jnp.float32
 BF16 = jnp.bfloat16
-Z_ORDER = (1, 3, 2, 0)
+EARLY = 2
 
 
 def row_sums(values):
@@ -247,6 +247,15 @@
         precision=lax.Precision.HIGHEST,
         preferred_element_type=F32,
     )
+
+
+def peer_block(dp, dz, ry, rx):
+    z, y, x = dp // 4, (dp // 2) % 2, dp % 2
+    return ((z + dz) % 4) * 4 + ((y + ry) % 2) * 2 + (x + rx) % 2
+
+
+def each(low, high, step):
+    lax.fori_loop(low, high, lambda i, carry: (step(i), carry)[1], 0)
 
 
 def window_kernel(
@@ -260,30 +269,28 @@
     width = cols * 16
     sec = lax.axis_index("section")
     dp = lax.axis_index("dp")
-    z, y, x = dp // 4, (dp // 2) % 2, dp % 2
-    px, py = dp + 1 - 2 * x, dp + 2 - 4 * y
+    px, py = peer_block(dp, 0, 0, 1), peer_block(dp, 0, 1, 0)
 
     def zp(dz):
-        return ((z + dz) % 4) * 4 + y * 2 + x
+        return peer_block(dp, dz, 0, 0)
 
     def block_cols(dz, ry, rx):
-        yy = 1 - y if ry else y
-        xx = 1 - x if rx else x
-        return pl.ds(pl.multiple_of((((z + dz) % 4) * 4 + yy * 2 + xx) * cols, cols), cols)
-
-    def send(src, dst, s_sem, r_sem, section, chip):
-        copy = pltpu.make_async_remote_copy(
+        return pl.ds(pl.multiple_of(peer_block(dp, dz, ry, rx) * cols, cols), cols)
+
+    def remote(src, dst, s_sem, r_sem, section, chip):
+        return pltpu.make_async_remote_copy(
             src_ref=src, dst_ref=dst, send_sem=s_sem, recv_sem=r_sem,
             device_id=(section, chip), device_id_type=MESH,
         )
-        copy.start()
-        return copy
+
+    def send(*args):
+        remote(*args).start()
 
     def arrived(dst, r_sem):
-        pltpu.make_async_remote_copy(
-            src_ref=dst, dst_ref=dst, send_sem=r_sem, recv_sem=r_sem,
-            device_id=(sec, dp), device_id_type=MESH,
-        ).wait_recv()
+        remote(dst, dst, r_sem, r_sem, sec, dp).wait_recv()
+
+    def sent(src, s_sem):
+        remote(src, src, s_sem, s_sem, sec, dp).wait_send()
 
     load_h = pltpu.make_async_copy(h0_hbm, h0, in_sem.at[0])
     load_h.start()
@@ -293,93 +300,130 @@
     load_w.start()
 
     barrier = pltpu.get_barrier_semaphore()
-    for step in range(1, 16):
-        pl.semaphore_signal(barrier, inc=1, device_id=(sec, (dp + step) % 16), device_id_type=MESH)
+
+    def greet(section, chip):
+        pl.semaphore_signal(barrier, inc=1, device_id=(section, chip), device_id_type=MESH)
+
+    each(1, 16, lambda step: greet(sec, (dp + step) % 16))
     for chip in (dp, px, py, zp(1), zp(2), zp(3)):
-        pl.semaphore_signal(barrier, inc=1, device_id=(1 - sec, chip), device_id_type=MESH)
+        greet(1 - sec, chip)
     pl.semaphore_wait(barrier, 21)
 
     def stat_send(k, value):
         stats[k, dp] = value[0:2]
-        copies = []
-        for step in range(1, 16):
-            copies.append(send(
-                stats.at[k, dp], stats.at[k, dp], st_s.at[k, step], st_r.at[k, step],
-                sec, (dp + step) % 16,
-            ))
-        return copies
+        each(1, 16, lambda step: send(
+            stats.at[k, dp], stats.at[k, dp], st_s.at[k, step], st_r.at[k, step],
+            sec, (dp + step) % 16,
+        ))
 
     def stat_total(k):
-        for step in range(1, 16):
-            arrived(stats.at[k, (dp + 16 - step) % 16], st_r.at[k, step])
+        each(1, 16, lambda step: arrived(stats.at[k, (dp + 16 - step) % 16], st_r.at[k, step]))
         total = jnp.sum(stats[k], axis=0)
         return jnp.transpose(jnp.concatenate([total] * 4, axis=0))
 
+    def stat_sent(k):
+        each(1, 16, lambda step: sent(stats.at[k, dp], st_s.at[k, step]))
+
     def gather_own(src, section, include_self):
-        copies = []
         for dz in (1, 2, 3):
-            copies.append(send(src, gf.at[4 - dz, 0, 0], own_s.at[dz], ag_r.at[4 - dz, 0], section, zp(dz)))
-        copies.append(send(src, gf.at[0, 0, 1], own_s.at[4], ag_r.at[0, 1], section, px))
-        copies.append(send(src, gf.at[0, 1, 0], own_s.at[5], ag_r.at[0, 2], section, py))
+            send(src, gf.at[4 - dz, 0, 0], own_s.at[dz], ag_r.at[4 - dz, 0], section, zp(dz))
+        send(src, gf.at[0, 0, 1], own_s.at[4], ag_r.at[0, 1], section, px)
+        send(src, gf.at[0, 1, 0], own_s.at[5], ag_r.at[0, 2], section, py)
         if include_self:
-            copies.append(send(src, gf.at[0, 0, 0], own_s.at[0], ag_r.at[0, 0], section, dp))
-        return copies
-
-    def gather_rest(use, own_arrives):
-        copies = []
-        for dz in (1, 3, 2):
-            arrived(gf.at[dz, 0, 0], ag_r.at[dz, 0])
-            copies.append(send(gf.at[dz, 0, 0], gf.at[dz, 0, 1], ag_s.at[dz, 0], ag_r.at[dz, 1], sec, px))
-            copies.append(send(gf.at[dz, 0, 0], gf.at[dz, 1, 0], ag_s.at[dz, 1], ag_r.at[dz, 2], sec, py))
-            if dz == 1:
-                if own_arrives:
+            send(src, gf.at[0, 0, 0], own_s.at[0], ag_r.at[0, 0], section, dp)
+
+    def own_sent(src, include_self):
+        each(0 if include_self else 1, 6, lambda k: sent(src, own_s.at[k]))
+
+    def kept(dz, ry, rx):
+        return pltpu.make_async_copy(
+            gf.at[dz, ry, rx], gf_hbm.at[dz, ry, rx], keep_sem.at[dz * 4 + ry * 2 + rx])
+
+    def use(dz, ry, rx):
+        kept(dz, ry, rx).start()
+        back[...] += lax.dot_general(
+            gf[dz, ry, rx], w[:, block_cols(dz, ry, rx)], (((1,), (1,)), ((), ())),
+            preferred_element_type=F32,
+        )
+
+    def gather_rest(own_arrives):
+        back[...] = jnp.zeros_like(back)
+
+        def along_z(i):
+            dz = (i + 1) % 4
+
+            @pl.when(dz != 0)
+            def _():
+                arrived(gf.at[dz, 0, 0], ag_r.at[dz, 0])
+                send(gf.at[dz, 0, 0], gf.at[dz, 0, 1], ag_s.at[dz, 0], ag_r.at[dz, 1], sec, px)
+                send(gf.at[dz, 0, 0], gf.at[dz, 1, 0], ag_s.at[dz, 1], ag_r.at[dz, 2], sec, py)
+
+            if own_arrives:
+                @pl.when(dz == 0)
+                def _():
                     arrived(gf.at[0, 0, 0], ag_r.at[0, 0])
-                use(0, 0, 0)
+
             use(dz, 0, 0)
-        for dz in (0, 1, 3, 2):
+
+        def across(dz):
             arrived(gf.at[dz, 0, 1], ag_r.at[dz, 1])
-            copies.append(send(
-                gf.at[dz, 0, 1, low], gf.at[dz, 1, 1, low], ag_s.at[dz, 2], ag_r.at[dz, 3], sec, py))
+            send(gf.at[dz, 0, 1, low], gf.at[dz, 1, 1, low], ag_s.at[dz, 2], ag_r.at[dz, 3], sec, py)
             arrived(gf.at[dz, 1, 0], ag_r.at[dz, 2])
-            copies.append(send(
-                gf.at[dz, 1, 0, high], gf.at[dz, 1, 1, high], ag_s.at[dz, 3], ag_r.at[dz, 4], sec, px))
-            use(dz, 0, 1)
-            use(dz, 1, 0)
-        for dz in (0, 1, 3, 2):
+            send(gf.at[dz, 1, 0, high], gf.at[dz, 1, 1, high], ag_s.at[dz, 3], ag_r.at[dz, 4], sec, px)
+            each(0, 2, lambda k: use(dz, k, 1 - k))
+
+        def diagonal(dz):
             arrived(gf.at[dz, 1, 1, low], ag_r.at[dz, 3])
             arrived(gf.at[dz, 1, 1, high], ag_r.at[dz, 4])
             use(dz, 1, 1)
-        return copies
-
-    def scatter_first(rows, order):
-        copies = []
-        for dz in order:
-            for ry, rx in ((0, 1), (1, 1), (1, 0), (0, 0)):
-                part[dz, ry, rx] = jnp.dot(
-                    rows[...], w[:, block_cols(dz, ry, rx)], preferred_element_type=F32
-                ).astype(BF16)
-                if (ry, rx) == (1, 1):
-                    copies.append(send(
-                        part.at[dz, pl.ds(0, 2), 1, low], a1.at[dz], rs_s.at[dz, 0], rs_r.at[dz, 0], sec, px))
-                if (ry, rx) == (1, 0):
-                    copies.append(send(
-                        part.at[dz, 1, pl.ds(0, 2), high], b1.at[dz], rs_s.at[dz, 1], rs_r.at[dz, 1], sec, py))
-        return copies
-
-    def scatter_second():
-        copies = []
-        for dz in Z_ORDER:
+
+        each(0, 4, along_z)
+        each(0, 4, across)
+        each(0, 4, diagonal)
+
+    def rest_sent():
+        def forwarded(dz):
+            sent(gf.at[dz, 0, 0], ag_s.at[dz, 0])
+            sent(gf.at[dz, 0, 0], ag_s.at[dz, 1])
+
+        def halves(dz):
+            sent(gf.at[dz, 0, 1, low], ag_s.at[dz, 2])
+            sent(gf.at[dz, 1, 0, high], ag_s.at[dz, 3])
+
+        each(1, 4, forwarded)
+        each(0, 4, halves)
+        each(0, 16, lambda k: kept(k // 4, (k // 2) % 2, k % 2).wait())
+
+    def scatter_first(rows, start, stop):
+        def step(k):
+            dz, j = (k // 4 + 1) % 4, k % 4
+            ry, rx = 1 - j % 2, 1 - j // 2
+            part[dz, ry, rx] = jnp.dot(
+                rows[...], w[:, block_cols(dz, ry, rx)], preferred_element_type=F32
+            ).astype(BF16)
+
+            @pl.when(j == 1)
+            def _():
+                send(part.at[dz, pl.ds(0, 2), 1, low], a1.at[dz], rs_s.at[dz, 0], rs_r.at[dz, 0], sec, px)
+
+            @pl.when(j == 2)
+            def _():
+                send(part.at[dz, 1, pl.ds(0, 2), high], b1.at[dz], rs_s.at[dz, 1], rs_r.at[dz, 1], sec, py)
+
+        each(4 * start, 4 * stop, step)
+
+    def scatter_rest(landing, r_sems, self_too):
+        def second(i):
+            dz = (i + 1) % 4
             arrived(a1.at[dz], rs_r.at[dz, 0])
             sa[dz] = (part[dz, 1, 0, low].astype(F32) + a1[dz, 1].astype(F32)).astype(BF16)
-            copies.append(send(sa.at[dz], a2.at[dz], rs_s.at[dz, 2], rs_r.at[dz, 2], sec, py))
+            send(sa.at[dz], a2.at[dz], rs_s.at[dz, 2], rs_r.at[dz, 2], sec, py)
             arrived(b1.at[dz], rs_r.at[dz, 1])
             sb[dz] = (part[dz, 0, 1, high].astype(F32) + b1[dz, 1].astype(F32)).astype(BF16)
-            copies.append(send(sb.at[dz], b2.at[dz], rs_s.at[dz, 3], rs_r.at[dz, 3], sec, px))
-        return copies
-
-    def scatter_third(landing, r_sems, self_too):
-        copies = []
-        for dz in Z_ORDER:
+            send(sb.at[dz], b2.at[dz], rs_s.at[dz, 3], rs_r.at[dz, 3], sec, px)
+
+        def third(i):
+            dz = (i + 1) % 4
             arrived(a2.at[dz], rs_r.at[dz, 2])
             tz[dz, low] = (
                 part[dz, 0, 0, low].astype(F32) + a1[dz, 0].astype(F32) + a2[dz].astype(F32)
@@ -388,23 +432,26 @@
             tz[dz, high] = (
                 part[dz, 0, 0, high].astype(F32) + b1[dz, 0].astype(F32) + b2[dz].astype(F32)
             ).astype(BF16)
-            if dz:
-                copies.append(send(tz.at[dz], landing.at[4 - dz], z_s.at[dz], r_sems.at[4 - dz], 1, zp(dz)))
-            elif self_too:
-                copies.append(send(tz.at[0], landing.at[0], z_s.at[0], r_sems.at[0], 1, dp))
-        return copies
-
-    def back_step(dz, ry, rx):
-        return lax.dot_general(
-            gf[dz, ry, rx], w[:, block_cols(dz, ry, rx)], (((1,), (1,)), ((), ())),
-            preferred_element_type=F32,
-        )
-
-    def keep(dz, ry, rx):
-        copy = pltpu.make_async_copy(
-            gf.at[dz, ry, rx], gf_hbm.at[dz, ry, rx], keep_sem.at[dz * 4 + ry * 2 + rx])
-        copy.start()
-        return copy
+            there = (4 - dz) % 4
+            if self_too:
+                send(tz.at[dz], landing.at[there], z_s.at[dz], r_sems.at[there], 1, zp(dz))
+            else:
+                @pl.when(dz != 0)
+                def _():
+                    send(tz.at[dz], landing.at[there], z_s.at[dz], r_sems.at[there], 1, zp(dz))
+
+        each(0, 4, second)
+        each(0, 4, third)
+
+    def scatter_sent(self_too):
+        def step(dz):
+            sent(part.at[dz, pl.ds(0, 2), 1, low], rs_s.at[dz, 0])
+            sent(part.at[dz, 1, pl.ds(0, 2), high], rs_s.at[dz, 1])
+            sent(sa.at[dz], rs_s.at[dz, 2])
+            sent(sb.at[dz], rs_s.at[dz, 3])
+
+        each(0, 4, step)
+        each(0 if self_too else 1, 4, lambda dz: sent(tz.at[dz], z_s.at[dz]))
 
     def scale_of(totals):
         return lax.rsqrt(totals[:, 0:1] / width + NORM_EPS)
@@ -418,71 +465,52 @@
     def _():
         load_h.wait()
         entered = h0[...].astype(F32)
-        copies = stat_send(0, row_sums(entered * entered))
+        stat_send(0, row_sums(entered * entered))
         load_w.wait()
-        copies += scatter_first(h0, Z_ORDER)
+        scatter_first(h0, 0, 4)
         load_c.wait()
-        copies += scatter_second()
-        copies += scatter_third(zra, za_r, True)
+        scatter_rest(zra, za_r, True)
         scale = scale_of(stat_total(0))
         set_normed(h0[...], scale)
-        back[...] = jnp.zeros_like(back)
-        writes = []
-
-        def use(dz, ry, rx):
-            back[...] += back_step(dz, ry, rx)
-            writes.append(keep(dz, ry, rx))
-
-        copies += gather_rest(use, True)
+        gather_rest(True)
         normed = nrm[...].astype(F32)
-        copies += stat_send(2, row_sums(back[...] * normed))
+        stat_send(2, row_sums(back[...] * normed))
         gu[...] = gf[0, 0, 0, high]
         arrived(ad, ex_r.at[0])
+        scatter_sent(True)
+        stat_sent(0)
+        rest_sent()
         dot = stat_total(2)[:, 0:1]
         own[...] = (
             gf[0, 0, 0].astype(F32) + scale * (back[...] - normed * dot / width)
         ).astype(BF16)
-        copies.append(send(own.at[high], gu, ex_s.at[0], ex_r.at[1], 1, dp))
+        send(own.at[high], gu, ex_s.at[0], ex_r.at[1], 1, dp)
         gd[...] = own[low]
         arrived(au, ex_r.at[2])
-        for copy in writes:
-            copy.wait()
-        for copy in copies:
-            copy.wait_send()
+        stat_sent(2)
+        sent(own.at[high], ex_s.at[0])
 
     @pl.when(sec == 1)
     def _():
         load_c.wait()
-        copies = gather_own(cot, 1, False)
+        gather_own(cot, 1, False)
         gf[0, 0, 0] = cot[...]
         load_h.wait()
         entered = h0[...].astype(F32)
-        copies += stat_send(0, row_sums(entered * entered))
-        back[...] = jnp.zeros_like(back)
+        stat_send(0, row_sums(entered * entered))
         load_w.wait()
-
-        writes = []
-
-        def use(dz, ry, rx):
-            back[...] += back_step(dz, ry, rx)
-            writes.append(keep(dz, ry, rx))
-
-        copies += gather_rest(use, False)
-        for copy in copies:
-            copy.wait_send()
+        gather_rest(False)
         scale = scale_of(stat_total(0))
-        for dz in (0, 1, 3, 2):
-            arrived(zra.at[dz], za_r.at[dz])
+        each(0, 4, lambda dz: arrived(zra.at[dz], za_r.at[dz]))
         mixed = (
             zra[0].astype(F32) + zra[1].astype(F32) + zra[2].astype(F32) + zra[3].astype(F32)
         )
-        hid[...] = (entered + scale * mixed).astype(BF16)
+        hid[...] = (h0[...].astype(F32) + scale * mixed).astype(BF16)
         hidden = hid[...].astype(F32)
         first = lax.broadcasted_iota(jnp.int32, (8, tok), 0) == 0
-        copies = stat_send(1, jnp.where(first, row_sums(hidden * hidden), row_sums(back[...] * hidden)))
-        copies += scatter_first(hid, Z_ORDER[:2])
-        copies.append(send(hid.at[low], ad, ex_s.at[0], ex_r.at[0], 0, dp))
-        au[...] = hid[high]
+        stat_send(1, jnp.where(first, row_sums(hidden * hidden), row_sums(back[...] * hidden)))
+        scatter_first(hid, 0, EARLY)
+        own_sent(cot, False)
         totals = stat_total(1)
         scale = scale_of(totals)
         dot = totals[:, 1:2] * scale
@@ -490,50 +518,60 @@
         own[...] = (
             cot[...].astype(F32) + scale * (back[...] - nrm[...].astype(F32) * dot / width)
         ).astype(BF16)
-        copies += gather_own(own, 0, True)
-        copies += scatter_first(hid, Z_ORDER[2:])
-        copies += scatter_second()
+        gather_own(own, 0, True)
+        scatter_first(hid, EARLY, 4)
+        send(hid.at[low], ad, ex_s.at[0], ex_r.at[0], 0, dp)
+        au[...] = hid[high]
         gd[...] = own[low]
-        copies += scatter_third(zrb, zb_r, False)
+        stat_sent(0)
+        rest_sent()
+        scatter_rest(zrb, zb_r, False)
         mixed = tz[0].astype(F32)
         for dz in (1, 2, 3):
             arrived(zrb.at[dz], zb_r.at[dz])
             mixed = mixed + zrb[dz].astype(F32)
         tz[0] = (hid[...].astype(F32) + scale * mixed).astype(BF16)
-        copies.append(send(tz.at[0, high], au, ex_s.at[1], ex_r.at[2], 0, dp))
+        send(tz.at[0, high], au, ex_s.at[1], ex_r.at[2], 0, dp)
         ad[...] = tz[0, low]
+        own_sent(own, True)
+        scatter_sent(False)
+        stat_sent(1)
+        sent(hid.at[low], ex_s.at[0])
+        sent(tz.at[0, high], ex_s.at[1])
         arrived(gu, ex_r.at[1])
-        for copy in writes:
-            copy.wait()
-        for copy in copies:
-            copy.wait_send()
-
-
-def finish_kernel(nrm_t, gf_hbm, *refs):
-    kept, outs, (wg_hbm, gf, wg, in_sem, wg_sem, out_sem) = refs[:4], refs[4:8], refs[8:]
+
+
+def finish_kernel(nrm_hbm, gf_hbm, *refs):
+    held, outs = refs[:4], refs[4:8]
+    wg_hbm, nrm_t, gf, wg, in_sem, wg_sem, out_sem = refs[8:]
     cols = nrm_t.shape[0]
     dp = lax.axis_index("dp")
-    z, y, x = dp // 4, (dp // 2) % 2, dp % 2
-    loads, copies = [], []
-    for k in range(16):
-        spot = (k // 4, (k // 2) % 2, k % 2)
-        loads.append(pltpu.make_async_copy(gf_hbm.at[spot], gf.at[k], in_sem.at[k]))
-        loads[k].start()
-    for k in range(4):
-        copies.append(pltpu.make_async_copy(kept[k], outs[k], out_sem.at[k]))
-        copies[k].start()
-    for k in range(16):
-        loads[k].wait()
-        yy = 1 - y if (k // 2) % 2 else y
-        xx = 1 - x if k % 2 else x
-        block = ((z + k // 4) % 4) * 4 + yy * 2 + xx
+
+    def load(k):
+        return pltpu.make_async_copy(gf_hbm.at[k // 4, (k // 2) % 2, k % 2], gf.at[k], in_sem.at[k])
+
+    def write(k):
+        spot = peer_block(dp, k // 4, (k // 2) % 2, k % 2) * cols
+        return pltpu.make_async_copy(
+            wg.at[k], wg_hbm.at[:, pl.ds(pl.multiple_of(spot, cols), cols)], wg_sem.at[k])
+
+    load_n = pltpu.make_async_copy(nrm_hbm, nrm_t, out_sem.at[4])
+    load_n.start()
+    each(0, 16, lambda k: load(k).start())
+    copies = [pltpu.make_async_copy(held[k], outs[k], out_sem.at[k]) for k in range(4)]
+    for copy in copies:
+        copy.start()
+    load_n.wait()
+
+    def step(k):
+        load(k).wait()
         wg[k] = jnp.dot(nrm_t[...], gf[k], preferred_element_type=F32)
-        spot = pl.ds(pl.multiple_of(block * cols, cols), cols)
-        copy = pltpu.make_async_copy(wg.at[k], wg_hbm.at[:, spot], wg_sem.at[k])
-        copy.start()
-        copies.append(copy)
+        write(k).start()
+
+    each(0, 16, step)
     for copy in copies:
         copy.wait()
+    each(0, 16, lambda k: write(k).wait())
 
 
 def direct_body(entering, cotangent, weights):
@@ -590,12 +628,13 @@
     *outs, weight_grad = pl.pallas_call(
         finish_kernel,
         out_shape=(half_out,) * 4 + (jax.ShapeDtypeStruct((cols, width), F32),),
-        in_specs=[vm, hbm] + [vm] * 4,
+        in_specs=[hbm] * 6,
         out_specs=(hbm,) * 5,
         scratch_shapes=[
+            pltpu.VMEM((cols, tok), BF16),
             pltpu.VMEM((16, tok, cols), BF16),
             pltpu.VMEM((16, cols, cols), F32),
-            dma((16,)), dma((16,)), dma((4,)),
+            dma((16,)), dma((16,)), dma((5,)),
         ],
         compiler_params=pltpu.CompilerParams(vmem_limit_bytes=63 * 1024 * 1024),
         cost_estimate=pl.CostEstimate(

time: 65.3 us -> 69.1 us (1.058)
  Pallas kernels: 64.4 us -> 68.4 us
    pallas_call x1, Pallas kernels: 6.48 us -> 9.7 us  [direct_body(): pl.pallas_call(finish_kernel, out_shape=(half_out,) * 4 + (jax.ShapeDtype...]
where the time goes in v3:
time: 69.1 us; the launch traced here: 69 us
  Pallas kernels  68.4 us (99%)
    pallas_call x1, Pallas kernels, direct_body(): pl.pallas_call(window_kernel, out_shape=(half_out,) * 4 + (jax.ShapeDtype...  58.7 us
    pallas_call x1, Pallas kernels, direct_body(): pl.pallas_call(finish_kernel, out_shape=(half_out,) * 4 + (jax.ShapeDtype...  9.7 us

profile of v3, /device:TPU:0, one launch (start us, length us, event | category | flops | bytes accessed | tf_op | source)
XLA Modules:
  0.0 69.0 jit_solution(2285694962077395030)
XLA Ops:
  0.6 58.7 %shard_map.74 = (bf16[128,256]{1,0:T(8,128)(2,1)}, bf16[128,256]{1,0:T(8,128)(2,1)}, bf16[128,256]{1,0:T(8,128)(2,1)}, bf16[128,256]{1,0:T(8,128)(2,1)}, bf16[25...) custom-call(bf16[256,256]{1,0:T(8,128)(2,1)} %bitcast.8, bf16[256,256]{1,0:T(8,128)(2,1)} %bitcast.9, ...), custom_call_target="tpu_custom_call" | custom-call | flops 1073741824 | bytes 4194304 | tf_op jit(solution)/shard_map/pallas_call | solution.py:588
  59.3 9.7 %shard_map.75 = (bf16[128,256]{1,0:T(8,128)(2,1)}, bf16[128,256]{1,0:T(8,128)(2,1)}, bf16[128,256]{1,0:T(8,128)(2,1)}, bf16[128,256]{1,0:T(8,128)(2,1)}, f32[256,4096]{1,0:T(8,128)}) custom-call(bf16[256,256]{1,0:T(8,128)(2,1)} %get-tuple-element.16.nrm_hbm, bf16[4,2,2,256,256]{4,3,2,1,0:T(8,128)(2,1)} %get-tuple-element.17.gf_hbm, ...), custom_call_target="tpu_custom_call" | custom-call | flops 536870912 | bytes 6291456 | tf_op jit(solution)/shard_map/pallas_call | solution.py:628

commit v4 on v3

--- a/solution.py
+++ b/solution.py
@@ -260,8 +260,8 @@
 
 def window_kernel(
     h0_hbm, cot_hbm, w_hbm, ad, au, gd, gu, nrm_t, gf_hbm,
-    h0, cot, w, gf, part, a1, b1, a2, b2, sa, sb, tz, zra, zrb, stats, back, hid, nrm, own,
-    in_sem, keep_sem, st_s, st_r, ag_s, ag_r, own_s, rs_s, rs_r, z_s, za_r, zb_r, ex_s, ex_r,
+    h0, cot, w, gf, part, a1, b1, a2, b2, sa, sb, tz, zra, zrb, stats, back, hid, nrm, own, grown,
+    early, e_s, e_r, in_sem, keep_sem, st_s, st_r, ag_s, ag_r, own_s, rs_s, rs_r, z_s, za_r, zb_r, ex_s, ex_r,
 ):
     tok, cols = h0.shape
     half = tok // 2
@@ -304,10 +304,39 @@
     def greet(section, chip):
         pl.semaphore_signal(barrier, inc=1, device_id=(section, chip), device_id_type=MESH)
 
-    each(1, 16, lambda step: greet(sec, (dp + step) % 16))
-    for chip in (dp, px, py, zp(1), zp(2), zp(3)):
-        greet(1 - sec, chip)
-    pl.semaphore_wait(barrier, 21)
+    for chip in (px, py, zp(1), zp(2), zp(3)):
+        greet(sec, chip)
+
+    @pl.when(sec == 1)
+    def _():
+        for chip in (dp, zp(1), zp(2), zp(3)):
+            greet(0, chip)
+
+    pl.semaphore_wait(barrier, 9 - 4 * sec)
+
+    def early_z(value):
+        early[0] = value[0:2]
+        for dz in (1, 2, 3):
+            send(early.at[0], early.at[4 - dz], e_s.at[dz], e_r.at[4 - dz], sec, zp(dz))
+
+    def early_y():
+        for dz in (1, 2, 3):
+            arrived(early.at[dz], e_r.at[dz])
+        early[6] = early[0] + early[1] + early[2] + early[3]
+        send(early.at[6], early.at[4], e_s.at[4], e_r.at[4], sec, py)
+
+    def early_x():
+        arrived(early.at[4], e_r.at[4])
+        early[7] = early[6] + early[4]
+        send(early.at[7], early.at[5], e_s.at[5], e_r.at[5], sec, px)
+
+    def early_total():
+        arrived(early.at[5], e_r.at[5])
+        each(1, 6, lambda k: sent(early.at[0], e_s.at[k]))
+        return columns(early[7] + early[5])
+
+    def columns(total):
+        return jnp.transpose(jnp.concatenate([total] * 4, axis=0))
 
     def stat_send(k, value):
         stats[k, dp] = value[0:2]
@@ -318,8 +347,7 @@
 
     def stat_total(k):
         each(1, 16, lambda step: arrived(stats.at[k, (dp + 16 - step) % 16], st_r.at[k, step]))
-        total = jnp.sum(stats[k], axis=0)
-        return jnp.transpose(jnp.concatenate([total] * 4, axis=0))
+        return columns(jnp.sum(stats[k], axis=0))
 
     def stat_sent(k):
         each(1, 16, lambda step: sent(stats.at[k, dp], st_s.at[k, step]))
@@ -346,7 +374,7 @@
             preferred_element_type=F32,
         )
 
-    def gather_rest(own_arrives):
+    def gather_rest(own_arrives, after_z=lambda: None, after_xy=lambda: None):
         back[...] = jnp.zeros_like(back)
 
         def along_z(i):
@@ -378,7 +406,9 @@
             use(dz, 1, 1)
 
         each(0, 4, along_z)
+        after_z()
         each(0, 4, across)
+        after_xy()
         each(0, 4, diagonal)
 
     def rest_sent():
@@ -412,7 +442,7 @@
 
         each(4 * start, 4 * stop, step)
 
-    def scatter_rest(landing, r_sems, self_too):
+    def scatter_rest(landing, r_sems, self_too, between=lambda: None):
         def second(i):
             dz = (i + 1) % 4
             arrived(a1.at[dz], rs_r.at[dz, 0])
@@ -441,6 +471,7 @@
                     send(tz.at[dz], landing.at[there], z_s.at[dz], r_sems.at[there], 1, zp(dz))
 
         each(0, 4, second)
+        between()
         each(0, 4, third)
 
     def scatter_sent(self_too):
@@ -465,29 +496,28 @@
     def _():
         load_h.wait()
         entered = h0[...].astype(F32)
-        stat_send(0, row_sums(entered * entered))
+        early_z(row_sums(entered * entered))
         load_w.wait()
         scatter_first(h0, 0, 4)
         load_c.wait()
-        scatter_rest(zra, za_r, True)
-        scale = scale_of(stat_total(0))
+        early_y()
+        scatter_rest(zra, za_r, True, early_x)
+        scale = scale_of(early_total())
         set_normed(h0[...], scale)
         gather_rest(True)
         normed = nrm[...].astype(F32)
-        stat_send(2, row_sums(back[...] * normed))
         gu[...] = gf[0, 0, 0, high]
         arrived(ad, ex_r.at[0])
         scatter_sent(True)
-        stat_sent(0)
         rest_sent()
-        dot = stat_total(2)[:, 0:1]
+        each(0, 16, lambda step: arrived(stats.at[1, (dp + 16 - step) % 16], st_r.at[1, step]))
+        dot = columns(jnp.sum(stats[1], axis=0))[:, 0:1]
         own[...] = (
             gf[0, 0, 0].astype(F32) + scale * (back[...] - normed * dot / width)
         ).astype(BF16)
         send(own.at[high], gu, ex_s.at[0], ex_r.at[1], 1, dp)
         gd[...] = own[low]
         arrived(au, ex_r.at[2])
-        stat_sent(2)
         sent(own.at[high], ex_s.at[0])
 
     @pl.when(sec == 1)
@@ -497,21 +527,22 @@
         gf[0, 0, 0] = cot[...]
         load_h.wait()
         entered = h0[...].astype(F32)
-        stat_send(0, row_sums(entered * entered))
+        early_z(row_sums(entered * entered))
         load_w.wait()
-        gather_rest(False)
-        scale = scale_of(stat_total(0))
+        gather_rest(False, early_y, early_x)
+        scale = scale_of(early_total())
         each(0, 4, lambda dz: arrived(zra.at[dz], za_r.at[dz]))
         mixed = (
             zra[0].astype(F32) + zra[1].astype(F32) + zra[2].astype(F32) + zra[3].astype(F32)
         )
-        hid[...] = (h0[...].astype(F32) + scale * mixed).astype(BF16)
+        grown[...] = scale * mixed
+        hid[...] = (h0[...].astype(F32) + grown[...]).astype(BF16)
         hidden = hid[...].astype(F32)
         first = lax.broadcasted_iota(jnp.int32, (8, tok), 0) == 0
-        stat_send(1, jnp.where(first, row_sums(hidden * hidden), row_sums(back[...] * hidden)))
+        stat_send(0, jnp.where(first, row_sums(hidden * hidden), row_sums(back[...] * hidden)))
         scatter_first(hid, 0, EARLY)
         own_sent(cot, False)
-        totals = stat_total(1)
+        totals = stat_total(0)
         scale = scale_of(totals)
         dot = totals[:, 1:2] * scale
         set_normed(hid[...], scale)
@@ -519,11 +550,13 @@
             cot[...].astype(F32) + scale * (back[...] - nrm[...].astype(F32) * dot / width)
         ).astype(BF16)
         gather_own(own, 0, True)
+        early[0] = row_sums(own[...].astype(F32) * grown[...])[0:2]
+        each(0, 16, lambda step: send(
+            early.at[0], stats.at[1, dp], st_s.at[1, step], st_r.at[1, step], 0, (dp + step) % 16))
         scatter_first(hid, EARLY, 4)
         send(hid.at[low], ad, ex_s.at[0], ex_r.at[0], 0, dp)
         au[...] = hid[high]
         gd[...] = own[low]
-        stat_sent(0)
         rest_sent()
         scatter_rest(zrb, zb_r, False)
         mixed = tz[0].astype(F32)
@@ -535,7 +568,8 @@
         ad[...] = tz[0, low]
         own_sent(own, True)
         scatter_sent(False)
-        stat_sent(1)
+        stat_sent(0)
+        each(0, 16, lambda step: sent(early.at[0], st_s.at[1, step]))
         sent(hid.at[low], ex_s.at[0])
         sent(tz.at[0, high], ex_s.at[1])
         arrived(gu, ex_r.at[1])
@@ -543,7 +577,7 @@
 
 def finish_kernel(nrm_hbm, gf_hbm, *refs):
     held, outs = refs[:4], refs[4:8]
-    wg_hbm, nrm_t, gf, wg, in_sem, wg_sem, out_sem = refs[8:]
+    wg_hbm, nrm_t, gf, wg, small, in_sem, wg_sem, held_sem, out_sem = refs[8:]
     cols = nrm_t.shape[0]
     dp = lax.axis_index("dp")
 
@@ -555,11 +589,12 @@
         return pltpu.make_async_copy(
             wg.at[k], wg_hbm.at[:, pl.ds(pl.multiple_of(spot, cols), cols)], wg_sem.at[k])
 
-    load_n = pltpu.make_async_copy(nrm_hbm, nrm_t, out_sem.at[4])
+    load_n = pltpu.make_async_copy(nrm_hbm, nrm_t, held_sem.at[4])
     load_n.start()
     each(0, 16, lambda k: load(k).start())
-    copies = [pltpu.make_async_copy(held[k], outs[k], out_sem.at[k]) for k in range(4)]
-    for copy in copies:
+    takes = [pltpu.make_async_copy(held[k], small.at[k], held_sem.at[k]) for k in range(4)]
+    copies = [pltpu.make_async_copy(small.at[k], outs[k], out_sem.at[k]) for k in range(4)]
+    for copy in takes:
         copy.start()
     load_n.wait()
 
@@ -569,6 +604,9 @@
         write(k).start()
 
     each(0, 16, step)
+    for take, copy in zip(takes, copies):
+        take.wait()
+        copy.start()
     for copy in copies:
         copy.wait()
     each(0, 16, lambda k: write(k).wait())
@@ -608,12 +646,14 @@
             pltpu.VMEM((4, tok, cols), BF16),
             pltpu.VMEM((4, tok, cols), BF16),
             pltpu.VMEM((4, tok, cols), BF16),
-            pltpu.VMEM((3, 16, 2, tok), F32),
+            pltpu.VMEM((2, 16, 2, tok), F32),
             pltpu.VMEM((tok, cols), F32),
             pltpu.VMEM((tok, cols), BF16),
             pltpu.VMEM((tok, cols), BF16),
             pltpu.VMEM((tok, cols), BF16),
-            dma((3,)), dma((16,)), dma((3, 16)), dma((3, 16)),
+            pltpu.VMEM((tok, cols), F32),
+            pltpu.VMEM((8, 2, tok), F32), dma((6,)), dma((6,)),
+            dma((3,)), dma((16,)), dma((2, 16)), dma((2, 16)),
             dma((4, 4)), dma((4, 5)), dma((6,)),
             dma((4, 4)), dma((4, 4)), dma((4,)), dma((4,)), dma((4,)),
             dma((2,)), dma((3,)),
@@ -634,7 +674,8 @@
             pltpu.VMEM((cols, tok), BF16),
             pltpu.VMEM((16, tok, cols), BF16),
             pltpu.VMEM((16, cols, cols), F32),
-            dma((16,)), dma((16,)), dma((5,)),
+            pltpu.VMEM((4, half, cols), BF16),
+            dma((16,)), dma((16,)), dma((5,)), dma((4,)),
         ],
         compiler_params=pltpu.CompilerParams(vmem_limit_bytes=63 * 1024 * 1024),
         cost_estimate=pl.CostEstimate(

time: 69.1 us -> 58.1 us (0.84)
  Pallas kernels: 68.4 us -> 57.3 us
    pallas_call x1, Pallas kernels: 58.7 us -> 52.1 us  [direct_body(): pl.pallas_call(window_kernel, out_shape=(half_out,) * 4 + (jax.ShapeDtype...]
    pallas_call x1, Pallas kernels: 9.7 us -> 5.26 us  [direct_body(): pl.pallas_call(finish_kernel, out_shape=(half_out,) * 4 + (jax.ShapeDtype...]
where the time goes in v4:
time: 58.1 us; the launch traced here: 58 us
  Pallas kernels  57.3 us (99%)
  between operations  0.64 us (1%)
    pallas_call x1, Pallas kernels, direct_body(): pl.pallas_call(window_kernel, out_shape=(half_out,) * 4 + (jax.ShapeDtype...  52.1 us
    pallas_call x1, Pallas kernels, direct_body(): pl.pallas_call(finish_kernel, out_shape=(half_out,) * 4 + (jax.ShapeDtype...  5.26 us

profile of v4, /device:TPU:0, one launch (start us, length us, event | category | flops | bytes accessed | tf_op | source)
XLA Modules:
  0.0 58.0 jit_solution(13017855039779889472)
XLA Ops:
  0.6 52.1 %shard_map.74 = (bf16[128,256]{1,0:T(8,128)(2,1)}, bf16[128,256]{1,0:T(8,128)(2,1)}, bf16[128,256]{1,0:T(8,128)(2,1)}, bf16[128,256]{1,0:T(8,128)(2,1)}, bf16[25...) custom-call(bf16[256,256]{1,0:T(8,128)(2,1)} %bitcast.8, bf16[256,256]{1,0:T(8,128)(2,1)} %bitcast.9, ...), custom_call_target="tpu_custom_call" | custom-call | flops 1073741824 | bytes 4194304 | tf_op jit(solution)/shard_map/pallas_call | solution.py:626
  52.7 5.3 %shard_map.75 = (bf16[128,256]{1,0:T(8,128)(2,1)}, bf16[128,256]{1,0:T(8,128)(2,1)}, bf16[128,256]{1,0:T(8,128)(2,1)}, bf16[128,256]{1,0:T(8,128)(2,1)}, f32[256,4096]{1,0:T(8,128)}) custom-call(bf16[256,256]{1,0:T(8,128)(2,1)} %get-tuple-element.16.nrm_hbm, bf16[4,2,2,256,256]{4,3,2,1,0:T(8,128)(2,1)} %get-tuple-element.17.gf_hbm, ...), custom_call_target="tpu_custom_call" | custom-call | flops 536870912 | bytes 6291456 | tf_op jit(solution)/shard_map/pallas_call | solution.py:668

commit v5 on v4

--- a/solution.py
+++ b/solution.py
@@ -235,7 +235,6 @@
 MESH = pl.DeviceIdType.MESH
 F32 = jnp.float32
 BF16 = jnp.bfloat16
-EARLY = 2
 
 
 def row_sums(values):
@@ -540,12 +539,12 @@
         hidden = hid[...].astype(F32)
         first = lax.broadcasted_iota(jnp.int32, (8, tok), 0) == 0
         stat_send(0, jnp.where(first, row_sums(hidden * hidden), row_sums(back[...] * hidden)))
-        scatter_first(hid, 0, EARLY)
+        scatter_first(hid, 0, 4)
         own_sent(cot, False)
         totals = stat_total(0)
         scale = scale_of(totals)
         dot = totals[:, 1:2] * scale
-        set_normed(hid[...], scale)
+        nrm[...] = (hid[...].astype(F32) * scale).astype(BF16)
         own[...] = (
             cot[...].astype(F32) + scale * (back[...] - nrm[...].astype(F32) * dot / width)
         ).astype(BF16)
@@ -553,7 +552,7 @@
         early[0] = row_sums(own[...].astype(F32) * grown[...])[0:2]
         each(0, 16, lambda step: send(
             early.at[0], stats.at[1, dp], st_s.at[1, step], st_r.at[1, step], 0, (dp + step) % 16))
-        scatter_first(hid, EARLY, 4)
+        nrm_t[...] = jnp.transpose(nrm[...].astype(F32)).astype(BF16)
         send(hid.at[low], ad, ex_s.at[0], ex_r.at[0], 0, dp)
         au[...] = hid[high]
         gd[...] = own[low]

time: 58.1 us -> 57.1 us (0.983)
  Pallas kernels: 57.3 us -> 56.3 us
    pallas_call x1, Pallas kernels: 52.1 us -> 51.1 us  [direct_body(): pl.pallas_call(window_kernel, out_shape=(half_out,) * 4 + (jax.ShapeDtype...]
where the time goes in v5:
time: 57.1 us; the launch traced here: 57 us
  Pallas kernels  56.3 us (99%)
  between operations  0.64 us (1%)
    pallas_call x1, Pallas kernels, direct_body(): pl.pallas_call(window_kernel, out_shape=(half_out,) * 4 + (jax.ShapeDtype...  51.1 us
    pallas_call x1, Pallas kernels, direct_body(): pl.pallas_call(finish_kernel, out_shape=(half_out,) * 4 + (jax.ShapeDtype...  5.26 us

profile of v5, /device:TPU:0, one launch (start us, length us, event | category | flops | bytes accessed | tf_op | source)
XLA Modules:
  0.0 57.0 jit_solution(831353530896970972)
XLA Ops:
  0.6 51.1 %shard_map.74 = (bf16[128,256]{1,0:T(8,128)(2,1)}, bf16[128,256]{1,0:T(8,128)(2,1)}, bf16[128,256]{1,0:T(8,128)(2,1)}, bf16[128,256]{1,0:T(8,128)(2,1)}, bf16[25...) custom-call(bf16[256,256]{1,0:T(8,128)(2,1)} %bitcast.8, bf16[256,256]{1,0:T(8,128)(2,1)} %bitcast.9, ...), custom_call_target="tpu_custom_call" | custom-call | flops 1073741824 | bytes 4194304 | tf_op jit(solution)/shard_map/pallas_call | solution.py:625
  51.7 5.3 %shard_map.75 = (bf16[128,256]{1,0:T(8,128)(2,1)}, bf16[128,256]{1,0:T(8,128)(2,1)}, bf16[128,256]{1,0:T(8,128)(2,1)}, bf16[128,256]{1,0:T(8,128)(2,1)}, f32[256,4096]{1,0:T(8,128)}) custom-call(bf16[256,256]{1,0:T(8,128)(2,1)} %get-tuple-element.16.nrm_hbm, bf16[4,2,2,256,256]{4,3,2,1,0:T(8,128)(2,1)} %get-tuple-element.17.gf_hbm, ...), custom_call_target="tpu_custom_call" | custom-call | flops 536870912 | bytes 6291456 | tf_op jit(solution)/shard_map/pallas_call | solution.py:667
